TPU v7x, 512 devices: a whole 4x8x8 slice. The times are simulated.
512 devices in a mesh: walk: 16 (over z, core), chol: 32 (over y, x).
Axes of the slice: x: 4, y: 8, z: 8, core: 2. Of those that a mesh axis runs over, the one named last changes fastest.
Arguments:
- phi_in: float32 [768, 28672], P('walk', 'chol'), may hold values from -0.6103301 to 0.6103301
- trial: float32 [512, 56], P('chol'), may hold values from -0.176776695 to 0.176776695
- lrot: bfloat16 [28672, 2048], P('chol'), may hold values from -0.0625 to 0.0625
- fields: float32 [2, 768, 2048], P(None, 'walk', 'chol'), may hold values from -6 to 6
- src_group: int32 [768, 1], replicated, may hold values from 0 to 15; in each aligned block of 48 rows (0 to 47, 48 to 95, ...) at most 6 rows name the same one
- src_slot: int32 [768], replicated, may hold values from 0 to 47
Outputs:
- phi_out: float32 [768, 28672], P('walk', 'chol')
- fbias: float32 [768, 2048], P('walk', 'chol')
Inputs may be any that keep to these rules, and one draw needn't show every extreme that they name: `src_group`: in each aligned block of 48 rows (the new walkers of one group) no group is named more than 6 times, a bound that some block reaches.
All inputs are finite; a program needn't handle non-finite values.
Results may differ from a plain program's by a relative error of at most 0.018.
Values may be sent and summed in bfloat16 or wider, within the bound.
No kernel may reach another device: no remote copies, remote signals or barrier semaphores. Data moves between devices by JAX's collectives and lax.ppermute only.
A program may use at most 64 MiB of HBM per device.

v0:
```python
import jax
import jax.numpy as jnp
from jax import lax
from jax.sharding import PartitionSpec as P


def invert_correlation(correlation):
    gram_matrix = jnp.einsum(
        "wki,wkj->wij", correlation, correlation, precision=lax.Precision.HIGHEST
    )
    factor = jnp.linalg.cholesky(gram_matrix)

    def solve_one(lower, matrix):
        return jax.scipy.linalg.cho_solve((lower, True), matrix.T)

    return jax.vmap(solve_one)(factor, correlation)


def body(phi_in, trial, lrot, fields, src_group, src_slot):
    groups = lax.axis_size("walk")
    own_group = lax.axis_index("walk")
    w_dev = phi_in.shape[0]
    row_width = phi_in.shape[1]
    orb_rows = trial.shape[0]
    elec_count = trial.shape[1]
    source_table = src_group.reshape(groups, w_dev)
    slot_table = src_slot.reshape(groups, w_dev)
    own_sources = lax.dynamic_index_in_dim(source_table, own_group, 0, keepdims=False)
    own_slots = lax.dynamic_index_in_dim(slot_table, own_group, 0, keepdims=False)
    wanted = own_sources * w_dev + own_slots
    piece_rows = lax.all_gather(phi_in, "walk", axis=0, tiled=True)
    positions = jnp.arange(piece_rows.shape[0], dtype=jnp.int32)
    selector = (wanted[:, None] == positions[None, :]).astype(jnp.float32)
    walkers = jnp.dot(selector, piece_rows, precision=lax.Precision.HIGHEST)
    walkers = walkers.reshape(w_dev, orb_rows, elec_count)
    local_count = fields.shape[2]
    chol_index = lax.axis_index("chol")
    fields_all = lax.all_gather(fields, "chol", axis=2, tiled=True)
    capped_local = jnp.zeros((w_dev, local_count), jnp.float32)
    for step_index in range(fields.shape[0]):
        partial_correlation = jnp.einsum(
            "ai,waj->wij", trial, walkers, precision=lax.Precision.HIGHEST
        )
        correlation = lax.psum(partial_correlation, "chol")
        inverse = invert_correlation(correlation)
        theta_half = jnp.einsum("wak,wkj->waj", walkers, inverse, precision=lax.Precision.HIGHEST)
        theta_half = theta_half.astype(jnp.bfloat16).reshape(w_dev, orb_rows * elec_count)
        partial_bias = jnp.dot(theta_half, lrot, preferred_element_type=jnp.float32)
        force_sum = lax.psum(partial_bias.astype(jnp.bfloat16), "chol").astype(jnp.float32)
        capped = jnp.clip(20.0 * force_sum, -1.0, 1.0)
        drive_field = (fields_all[step_index] - capped).astype(jnp.bfloat16)
        capped_local = lax.dynamic_slice_in_dim(capped, chol_index * local_count, local_count, 1)
        push_term = lax.dot_general(
            drive_field, lrot, (((1,), (1,)), ((), ())), preferred_element_type=jnp.float32
        )
        push_term = push_term.reshape(w_dev, orb_rows, elec_count)
        walkers = walkers + 0.03 * jnp.einsum(
            "wai,wij->waj", push_term, correlation, precision=lax.Precision.HIGHEST
        )
    return (walkers.reshape(w_dev, row_width), capped_local)


def solution(mesh):
    return jax.shard_map(
        body,
        mesh=mesh,
        in_specs=(
            P("walk", "chol"),
            P("chol", None),
            P("chol", None),
            P(None, "walk", "chol"),
            P(),
            P(),
        ),
        out_specs=(P("walk", "chol"), P("walk", "chol")),
        check_vma=False,
    )
```

profile of v0, /device:TPU:16, one launch (start us, length us, event | category | flops | bytes accessed | tf_op | source)
XLA Modules:
  0.0 1352.7 jit_solution(8703008998679900662)
XLA Ops:
  9.5 49.0 %all-gather.2.cloned.1.call-done = f32[768,896]{1,0:T(8,128)} async-done(((f32[48,896]{1,0:T(8,128)}), f32[768,896]{1,0:T(8,128)}) %all-gather.2.cloned.1.call-update) | async-done | bytes 2752528 | tf_op jit(solution)/shard_map/all_gather | solution.py:31
  58.5 2.9 fusion.17
  61.7 3.4 convolution_bitcast_fusion.1
  65.4 58.2 %all_gather.7 = f32[2,48,2048]{1,0,2:T(2,128)} all-gather(f32[2,48,64]{1,0,2:T(2,128)S(1)} %copy.18), channel_id=1, replica_groups=mesh['walk'=16,'chol'=32] {'chol'}, dimensions={2}, use_global_device_ids=true | all-gather | bytes 811008 | tf_op jit(solution)/shard_map/all_gather | solution.py:38
  123.5 102.2 %all-reduce.5.cloned.1.call-done = f32[48,56,56]{1,2,0:T(8,128)} async-done(((f32[48,56,56]{1,2,0:T(8,128)}), f32[48,56,56]{1,2,0:T(8,128)}) %all-reduce.5.cloned.1.call-update) | async-done | bytes 602128 | tf_op jit(solution)/shard_map/psum | solution.py:44
  225.7 4.2 fusion.31
  231.6 248.1 %custom-call.10 = f32[48,56,56]{2,1,0:T(8,128)} custom-call(f32[48,56,56]{2,1,0:T(8,128)} %fusion.5), custom_call_target="Cholesky" | custom-call | tf_op jit(solution)/shard_map/jit(cholesky)/cholesky | solution.py:11
  479.7 1.8 copy.22
  483.8 49.7 %custom-call.11 = f32[48,1,56,56]{0,2,3,1:T(8,128)} custom-call(f32[48,1,56,56]{0,3,2,1:T(8,128)} %select_bitcast_fusion.1), custom_call_target="InvertDiagBlocksLowerTriangular" | custom-call | tf_op jit(solution)/shard_map/vmap(jit(_cho_solve))/triangular_solve | solution.py:14
  533.5 2.0 copy.33
  535.6 2.5 fusion.3
  538.1 2.4 fusion.32
  542.7 3.7 convolution_convert_fusion.1
  546.5 2.8 fusion.30
  549.3 2.3 copy.39
  551.6 146.3 %all-reduce.7.cloned.1.call-done = bf16[48,2048]{1,0:T(8,128)(2,1)} async-done(((bf16[48,2048]{1,0:T(8,128)(2,1)}), bf16[48,2048]{1,0:T(8,128)(2,1)}) %all-reduce.7.cloned.1.call-update) | async-done | bytes 196624 | tf_op jit(solution)/shard_map/psum | solution.py:49
  697.9 3.4 fusion.10
  701.6 2.2 fusion.7
  703.9 3.4 convolution_bitcast_fusion
  707.4 159.3 %all-reduce.9.cloned.1.call-done = f32[48,56,56]{1,2,0:T(8,128)} async-done(((f32[48,56,56]{1,2,0:T(8,128)}), f32[48,56,56]{1,2,0:T(8,128)}) %all-reduce.9.cloned.1.call-update) | async-done | bytes 602128 | tf_op jit(solution)/shard_map/psum | solution.py:44
  866.7 4.2 fusion.33
  872.5 248.1 %custom-call.12 = f32[48,56,56]{2,1,0:T(8,128)} custom-call(f32[48,56,56]{2,1,0:T(8,128)} %fusion.2), custom_call_target="Cholesky" | custom-call | tf_op jit(solution)/shard_map/jit(cholesky)/cholesky | solution.py:11
  1120.6 1.8 copy.28
  1123.2 1.6 select_bitcast_fusion
  1124.8 49.7 %custom-call.13 = f32[48,1,56,56]{0,2,3,1:T(8,128)} custom-call(f32[48,1,56,56]{0,3,2,1:T(8,128)} %select_bitcast_fusion), custom_call_target="InvertDiagBlocksLowerTriangular" | custom-call | tf_op jit(solution)/shard_map/vmap(jit(_cho_solve))/triangular_solve | solution.py:14
  1174.5 2.0 copy.37
  1176.5 2.5 fusion
  1179.1 2.4 fusion.34
  1183.1 3.6 convolution_convert_fusion
  1187.5 150.6 %all-reduce.11.cloned.1.call-done = bf16[48,2048]{1,0:T(8,128)(2,1)} async-done(((bf16[48,2048]{1,0:T(8,128)(2,1)}), bf16[48,2048]{1,0:T(8,128)(2,1)}) %all-reduce.11.cloned.1.call-update) | async-done | bytes 196624 | tf_op jit(solution)/shard_map/psum | solution.py:49
  1338.2 3.4 fusion.12
  1341.8 2.2 fusion.6
  (55 shorter events, 16.0 us)
Async XLA Ops:
  7.2 54.6 %copy-start = (f32[16,56]{1,0:T(8,128)S(1)}, f32[16,56]{1,0:T(8,128)}, u32[]{:S(2)}) copy-start(f32[16,56]{1,0:T(8,128)} %param.10) | copy-start | bytes 10756
  7.2 51.3 %all-gather.2.cloned.1.call-start = ((), (), s32[]{:S(2)}) async-start(), calls=%async_computation | async-start | bytes 2924544 | tf_op jit(solution)/shard_map/all_gather | solution.py:31
  7.9 217.8 %all-reduce.5.cloned.1.call-start = ((), (), s32[]{:S(2)}) async-start(), calls=%async_computation.1 | async-start | bytes 2752512 | tf_op jit(solution)/shard_map/psum | solution.py:44
  61.7 478.8 %copy-start.4 = (f32[48,16,56]{2,1,0:T(8,128)}, f32[48,16,56]{2,1,0:T(8,128)S(1)}, u32[]{:S(2)}) copy-start(f32[48,16,56]{2,1,0:T(8,128)S(1)} %reshape.54) | copy-start | bytes 516100
  61.7 3.5 copy-start.8
  65.2 632.8 %all-reduce.7.cloned.1.call-start = ((), (), s32[]{:S(2)}) async-start(), calls=%async_computation.2 | async-start | bytes 393216 | tf_op jit(solution)/shard_map/psum | solution.py:49
  533.5 2.1 copy-start.2
  542.7 3.8 copy-start.3
  546.4 320.2 %all-reduce.9.cloned.1.call-start = ((), (), s32[]{:S(2)}) async-start(), calls=%async_computation.3 | async-start | bytes 2752512 | tf_op jit(solution)/shard_map/psum | solution.py:44
  551.6 150.0 %copy-start.5 = (f32[48,16,56]{2,1,0:T(8,128)S(1)}, f32[48,16,56]{2,1,0:T(8,128)}, u32[]{:S(2)}) copy-start(f32[48,16,56]{2,1,0:T(8,128)} %copy-done.4) | copy-start | bytes 516100
  707.3 630.8 %all-reduce.11.cloned.1.call-start = ((), (), s32[]{:S(2)}) async-start(), calls=%async_computation.4 | async-start | bytes 393216 | tf_op jit(solution)/shard_map/psum | solution.py:49
  1174.5 2.1 copy-start.1
  1183.0 3.6 copy-start.6
  1341.8 3.1 copy-start.7
Sparse Core Ops, SparseCore 0:
  10.1 48.3 all-gather.1
  65.3 160.3 all-reduce.4
  546.6 151.3 all-reduce.6
  707.4 159.1 all-reduce.8
  1186.8 151.3 all-reduce.10
where the time goes:
time: 1360 us; the launch traced here: 1350 us
  waiting for transfers between devices  608 us (45%)
  other arithmetic  603 us (44%)
  blocking collectives  58.2 us (4%)
  matrix products  49.2 us (4%)
  local copies, waits for them, and re-layouts  19 us (1%)
  between operations  14.6 us (1%)
    another operation x7, other arithmetic, invert_correlation(): factor = jnp.linalg.cholesky(gram_matrix)  498 us
    psum x2, waiting for transfers between devices, body(): lax.psum(partial_bias.astype(jnp.bfloat16), 'chol').astype(jnp.float32)  297 us
    psum x2, waiting for transfers between devices, body(): correlation = lax.psum(partial_correlation, 'chol')  261 us
    another operation x5, other arithmetic, solve_one(): return jax.scipy.linalg.cho_solve((lower, True), matrix.T)  103 us
    all_gather x1, blocking collectives, body(): fields_all = lax.all_gather(fields, 'chol', axis=2, tiled=True)  58.2 us
    all_gather x1, waiting for transfers between devices, body(): piece_rows = lax.all_gather(phi_in, 'walk', axis=0, tiled=True)  49 us
  transfers between devices with their start and end apart: 5, of which 5 were waited for; matrix products, arithmetic and copies ran while one was open for 1% of the time, Pallas kernels for 0%

commit v1 on v0

v1 whole, which is shorter than its diff:
```python
import jax
import jax.numpy as jnp
from jax import lax
from jax.experimental import pallas as pl
from jax.experimental.pallas import tpu as pltpu
from jax.sharding import PartitionSpec as P

F32 = jnp.float32
BF16 = jnp.bfloat16
LANES = 128
HALF = 64
ELECS = 56
ORBS = 16
TILES = 7
DEVS = 32
WALKERS = 48
OWNERS = 24
CAP = 6
CHOLS = 2048
TAU = 0.03
EXACT = lax.Precision.HIGHEST


def vmem(count=1):
    return [pl.BlockSpec(memory_space=pltpu.VMEM)] * count


def smem():
    return [pl.BlockSpec(memory_space=pltpu.SMEM)]


def lane_ids(rows):
    return lax.broadcasted_iota(jnp.int32, (rows, LANES), 1)


def turn(block, shift):
    shift = shift % LANES
    return pltpu.roll(block, shift, 1) if shift else block


def exact_dot(left, right, left_dim, right_dim):
    return lax.dot_general(
        left, right, (((left_dim,), (right_dim,)), ((), ())),
        precision=EXACT, preferred_element_type=F32,
    )


def take_orbital(tiles, orbital, dest, lanes):
    tile, offset = divmod(orbital * ELECS, LANES)
    shift = dest - offset
    low = turn(tiles[tile], shift)
    if offset + ELECS <= LANES:
        return low
    return jnp.where(lanes >= dest + LANES - offset, turn(tiles[tile + 1], shift), low)


def pack_pair(first, second, lanes):
    blocks = []
    for orbital in range(ORBS):
        left = take_orbital(first, orbital, 0, lanes)
        right = take_orbital(second, orbital, HALF, lanes)
        block = jnp.where(lanes < HALF, left, right)
        blocks.append(jnp.where((lanes & (HALF - 1)) < ELECS, block, 0.0))
    return blocks


def unpack_tile(blocks, tile, half, lanes):
    start = tile * LANES
    result = None
    for orbital in range(start // ELECS, (start + LANES - 1) // ELECS + 1):
        moved = turn(blocks[orbital], orbital * ELECS - start - half * HALF)
        if result is None:
            result = moved
        else:
            result = jnp.where(lanes >= orbital * ELECS - start, moved, result)
    return result


def block_diagonal(pair, lanes):
    return jnp.concatenate(
        [jnp.where(lanes < HALF, pair, 0.0), jnp.where(lanes >= HALF, pair, 0.0)], axis=0
    )


def invert_pair(gram):
    lanes = lane_ids(ELECS)
    row_ids = lax.broadcasted_iota(jnp.int32, (ELECS, LANES), 0)
    within = lanes & (HALF - 1)
    for k in range(ELECS):
        column = jnp.where(
            lanes < HALF,
            jnp.broadcast_to(gram[:, k:k + 1], (ELECS, LANES)),
            jnp.broadcast_to(gram[:, HALF + k:HALF + k + 1], (ELECS, LANES)),
        )
        pivot = column[k:k + 1, :]
        row = jnp.where(within[k:k + 1, :] == k, 1.0, gram[k:k + 1, :]) / pivot
        gram = jnp.where(within == k, 0.0, gram) - column * row
        gram = jnp.where(row_ids == k, jnp.broadcast_to(row, (ELECS, LANES)), gram)
    return gram


def correlate(trial, walkers):
    rows = DEVS * ORBS // 2
    low = exact_dot(trial, walkers[:rows], 0, 0)
    high = exact_dot(trial, walkers[rows:], 0, 0)
    return low[:HALF] + high[HALF:]


def theta_blocks(walkers, correlation):
    lanes = lane_ids(HALF)
    gram = exact_dot(correlation, correlation, 0, 0)
    packed = jnp.where(lanes[:ELECS] < HALF, gram[:ELECS], gram[HALF:HALF + ELECS])
    inverse_gram = invert_pair(packed)
    inverse_gram = jnp.concatenate([inverse_gram, jnp.zeros((HALF - ELECS, LANES), F32)], axis=0)
    inverse = exact_dot(block_diagonal(inverse_gram, lanes), block_diagonal(correlation, lanes), 1, 1)
    theta = exact_dot(walkers, inverse, 1, 0)
    return [theta[DEVS * a:DEVS * (a + 1)] for a in range(ORBS)]


def migrate_pack(table_ref, phi_ref, out_ref, rows_ref):
    for tile in range(TILES):
        rows_ref[:, tile, :] = phi_ref[:, tile * LANES:(tile + 1) * LANES]
    rows_ref[:, TILES, :] = jnp.zeros((WALKERS, LANES), F32)
    for j in range(out_ref.shape[0]):
        out_ref[j] = rows_ref[table_ref[j]]


def owner_pack(place_ref, rows_ref, trial_ref, out_ref, pad_ref):
    pad_ref[...] = jnp.zeros_like(pad_ref)
    pad_ref[:, :ELECS] = trial_ref[...]
    trial = pad_ref[0:8, :] + turn(pad_ref[8:16, :], HALF)
    for d in range(DEVS):
        if d < OWNERS:
            out_ref[d, 0:8, :] = rows_ref[place_ref[d]]
            out_ref[d, 8:16, :] = rows_ref[place_ref[d + OWNERS]]
        else:
            out_ref[d, 0:16, :] = jnp.zeros((16, LANES), F32)
        out_ref[d, 16:24, :] = trial


def store_theta(theta, wide_ref, out_ref):
    lanes = lane_ids(DEVS)
    for half in range(2):
        for tile in range(TILES):
            wide_ref[:, 8 * half + tile, :] = unpack_tile(theta, tile, half, lanes)
        wide_ref[:, 8 * half + TILES, :] = jnp.zeros((DEVS, LANES), F32)
    out_ref[:, 0:16, :] = wide_ref[...].astype(BF16)


def owner_first(in_ref, theta_ref, phi_ref, corr_ref, trial_ref, wide_ref):
    lanes = lane_ids(DEVS)
    tiles = [[in_ref[:, 8 * h + k, :] for k in range(TILES)] for h in range(2)]
    walkers = jnp.concatenate(pack_pair(tiles[0], tiles[1], lanes), axis=0)
    trial = jnp.concatenate([in_ref[:, 16 + k, :] for k in range(8)], axis=0)
    correlation = correlate(trial, walkers)
    phi_ref[...] = walkers
    corr_ref[...] = correlation
    trial_ref[...] = trial
    store_theta(theta_blocks(walkers, correlation), wide_ref, theta_ref)


def owner_next(push_ref, phi_ref, corr_ref, trial_ref, out_ref, wide_ref):
    lanes = lane_ids(DEVS)
    tiles = [[push_ref[:, 8 * h + k, :] for k in range(TILES)] for h in range(2)]
    push = jnp.concatenate(pack_pair(tiles[0], tiles[1], lanes), axis=0)
    old = block_diagonal(corr_ref[...], lane_ids(HALF))
    walkers = phi_ref[...] + TAU * exact_dot(push, old, 1, 0)
    correlation = correlate(trial_ref[...], walkers)
    theta = theta_blocks(walkers, correlation)
    store_theta(theta, wide_ref, out_ref)
    blocks = [walkers[DEVS * a:DEVS * (a + 1)] for a in range(ORBS)]
    for half in range(2):
        for tile in range(TILES):
            wide_ref[:, 8 * half + tile, :] = unpack_tile(blocks, tile, half, lanes)
    high = wide_ref[...].astype(BF16)
    out_ref[:, 16:32, :] = high
    out_ref[:, 32:48, :] = (wide_ref[...] - high.astype(F32)).astype(BF16)
    sent = correlation.astype(BF16)
    for d in range(DEVS):
        out_ref[d, 48:112, :] = sent


def force_kernel(theta_ref, lrot_ref, out_ref, wide_ref):
    wide_ref[...] = theta_ref[0:OWNERS, 0:16, :].astype(F32)
    theta = jnp.concatenate(
        [
            jnp.concatenate([wide_ref[:, 8 * h + k, :] for k in range(TILES)], axis=1)
            for h in range(2)
        ],
        axis=0,
    ).astype(BF16)
    force = jnp.dot(theta, lrot_ref[...], preferred_element_type=F32)
    force = jnp.concatenate([force, jnp.zeros((16, CHOLS), F32)], axis=0)
    lanes = lane_ids(32)
    for pair in range(DEVS // 2):
        block = force[:, pair * LANES:(pair + 1) * LANES]
        top, low = block[:32], block[32:]
        out_ref[2 * pair] = jnp.where(lanes < HALF, top, turn(low, HALF)).astype(BF16)
        out_ref[2 * pair + 1] = jnp.where(lanes < HALF, turn(top, HALF), low).astype(BF16)


def drive_kernel(step, force_ref, fields_ref, out_ref, capped_ref, pad_ref):
    total = force_ref[0].astype(F32)
    for c in range(1, DEVS):
        total = total + force_ref[c].astype(F32)
    capped = jnp.clip(20.0 * total, -1.0, 1.0)
    pad_ref[...] = jnp.zeros_like(pad_ref)
    pad_ref[0:WALKERS, 0:HALF] = fields_ref[step]
    lanes = lane_ids(32)
    fields = jnp.where(lanes < HALF, pad_ref[0:32, :], turn(pad_ref[32:64, :], HALF))
    drive = (fields - capped).astype(BF16)
    for d in range(DEVS):
        out_ref[d] = drive
    capped_ref[0:32, :] = capped[:, 0:HALF]
    capped_ref[32:WALKERS, :] = turn(capped, HALF)[0:WALKERS - 32, 0:HALF]


def gather_push(drive_ref, lrot_ref):
    lanes = lane_ids(32)
    tops, lows = [], []
    for pair in range(DEVS // 2):
        left = drive_ref[2 * pair].astype(F32)
        right = drive_ref[2 * pair + 1].astype(F32)
        tops.append(jnp.where(lanes < HALF, left, turn(right, HALF)))
        lows.append(jnp.where(lanes < HALF, turn(left, HALF), right)[0:16])
    drive = jnp.concatenate(
        [jnp.concatenate(tops, axis=1), jnp.concatenate(lows, axis=1)], axis=0
    ).astype(BF16)
    return lax.dot_general(
        drive, lrot_ref[...], (((1,), (1,)), ((), ())), preferred_element_type=F32
    )


def push_kernel(drive_ref, lrot_ref, out_ref):
    push = gather_push(drive_ref, lrot_ref)
    for half in range(2):
        rows = push[OWNERS * half:OWNERS * (half + 1)]
        for tile in range(TILES):
            out_ref[0:OWNERS, 8 * half + tile, :] = rows[:, tile * LANES:(tile + 1) * LANES]
        out_ref[0:OWNERS, 8 * half + TILES, :] = jnp.zeros((OWNERS, LANES), F32)
    out_ref[OWNERS:, :, :] = jnp.zeros((DEVS - OWNERS, 16, LANES), F32)


def last_kernel(drive_ref, lrot_ref, bundle_ref, out_ref, push_ref, wide_ref):
    push = gather_push(drive_ref, lrot_ref)
    lanes = lane_ids(OWNERS)
    tiles = [
        [
            push[OWNERS * h:OWNERS * (h + 1), k * LANES:(k + 1) * LANES]
            for k in range(TILES)
        ]
        for h in range(2)
    ]
    blocks = pack_pair(tiles[0], tiles[1], lanes)
    for orbital in range(ORBS):
        push_ref[:, orbital, :] = blocks[orbital]
    square = lane_ids(HALF)
    for d in range(OWNERS):
        pair = block_diagonal(bundle_ref[d, 48:112, :].astype(F32), square).astype(BF16)
        rows = push_ref[d]
        high = rows.astype(BF16)
        low = (rows - high.astype(F32)).astype(BF16)
        push_ref[d] = TAU * (
            jnp.dot(high, pair, preferred_element_type=F32)
            + jnp.dot(low, pair, preferred_element_type=F32)
        )
    moved = [push_ref[:, orbital, :] for orbital in range(ORBS)]
    wide_ref[...] = bundle_ref[0:OWNERS, 16:32, :].astype(F32) + bundle_ref[0:OWNERS, 32:48, :].astype(F32)
    for half in range(2):
        for tile in range(TILES):
            out_ref[OWNERS * half:OWNERS * (half + 1), tile * LANES:(tile + 1) * LANES] = (
                wide_ref[:, 8 * half + tile, :] + unpack_tile(moved, tile, half, lanes)
            )


def call(kernel, name, shapes, operands, in_specs, scratch=(), limit=48):
    single = not isinstance(shapes, (list, tuple))
    listed = [shapes] if single else list(shapes)
    result = pl.pallas_call(
        kernel,
        out_shape=listed,
        in_specs=in_specs,
        out_specs=vmem(len(listed)),
        scratch_shapes=list(scratch),
        compiler_params=pltpu.CompilerParams(vmem_limit_bytes=limit * 1024 * 1024),
        name=name,
    )(*operands)
    return result[0] if single else result


def shape(dims, dtype=F32):
    return jax.ShapeDtypeStruct(dims, dtype)


def exchange(array, axis):
    flat = array.reshape(-1, LANES)
    return lax.all_to_all(flat, axis, 0, 0, tiled=True).reshape(array.shape)


def tables(src_group, src_slot, groups, own_group, cap):
    source = src_group.reshape(groups, WALKERS)
    slots = src_slot.reshape(groups, WALKERS)
    order = jnp.arange(WALKERS, dtype=jnp.int32)
    earlier = (source[:, None, :] == source[:, :, None]) & (order[None, None, :] < order[None, :, None])
    rank = jnp.sum(earlier.astype(jnp.int32), axis=2)
    picked = (source == own_group)[:, None, :] & (
        rank[:, None, :] == jnp.arange(cap, dtype=jnp.int32)[None, :, None]
    )
    send = jnp.sum(jnp.where(picked, slots[:, None, :], 0), axis=2).reshape(groups * cap)
    own_source = lax.dynamic_index_in_dim(source, own_group, 0, keepdims=False)
    own_rank = lax.dynamic_index_in_dim(rank, own_group, 0, keepdims=False)
    return send.astype(jnp.int32), (own_source * cap + own_rank).astype(jnp.int32)


def body(phi_in, trial, lrot, fields, src_group, src_slot, cap=CAP):
    groups = lax.axis_size("walk")
    send, place = tables(src_group, src_slot, groups, lax.axis_index("walk"), cap)
    rows = call(
        migrate_pack, "migrate_pack", shape((groups * cap, 8, LANES)), (send, phi_in),
        smem() + vmem(), [pltpu.VMEM((WALKERS, 8, LANES), F32)],
    )
    rows = exchange(rows, "walk")
    owned = call(
        owner_pack, "owner_pack", shape((DEVS, 24, LANES)), (place, rows, trial),
        smem() + vmem(2), [pltpu.VMEM((ORBS, LANES), F32)],
    )
    owned = exchange(owned, "chol")
    wide = pltpu.VMEM((DEVS, 16, LANES), F32)
    few = pltpu.VMEM((OWNERS, 16, LANES), F32)
    theta, phi, corr, trial_all = call(
        owner_first, "owner_first",
        [
            shape((DEVS, 16, LANES), BF16), shape((DEVS * ORBS, LANES)),
            shape((HALF, LANES)), shape((DEVS * ORBS // 2, LANES)),
        ],
        (owned,), vmem(), [wide],
    )
    theta = exchange(theta, "chol")

    def forces(theta, step):
        force = call(
            force_kernel, "force", shape((DEVS, 32, LANES), BF16), (theta, lrot), vmem(2), [few]
        )
        force = exchange(force, "chol")
        drive, capped = call(
            lambda *refs: drive_kernel(step, *refs), "drive",
            [shape((DEVS, 32, LANES), BF16), shape((WALKERS, HALF))],
            (force, fields), vmem(2), [pltpu.VMEM((64, LANES), F32)],
        )
        return exchange(drive, "chol"), capped

    drive, _ = forces(theta, 0)
    push = call(push_kernel, "push", shape((DEVS, 16, LANES)), (drive, lrot), vmem(2))
    push = exchange(push, "chol")
    bundle = call(
        owner_next, "owner_next", shape((DEVS, 112, LANES), BF16),
        (push, phi, corr, trial_all), vmem(4), [wide],
    )
    bundle = exchange(bundle, "chol")
    drive, capped = forces(bundle, 1)
    phi_out = call(
        last_kernel, "last", shape((WALKERS, ORBS * ELECS)), (drive, lrot, bundle), vmem(3),
        [few, few],
    )
    return phi_out, capped


def solution(mesh):
    return jax.shard_map(
        body,
        mesh=mesh,
        in_specs=(
            P("walk", "chol"),
            P("chol", None),
            P("chol", None),
            P(None, "walk", "chol"),
            P(),
            P(),
        ),
        out_specs=(P("walk", "chol"), P("walk", "chol")),
        check_vma=False,
    )
```

time: 1360 us -> 198 us (0.15)
  the two profiles are of different devices: /device:TPU:16 before, /device:TPU:8 now
where the time goes in v1:
time: 198 us
  blocking collectives  143 us (72%)
  Pallas kernels  23.4 us (12%)
  waiting for transfers between devices  13.7 us (7%)
  starting transfers between devices  10.6 us (5%)
  local copies, waits for them, and re-layouts  4.68 us (2%)
    all_to_all x8, blocking collectives, exchange(): return lax.all_to_all(flat, axis, 0, 0, tiled=True).reshape(array.shape)  143 us
    pallas_call x10, Pallas kernels, call(): pl.pallas_call(kernel, out_shape=listed, in_specs=in_specs, out_specs=vme...  23.4 us
    all_to_all x1, waiting for transfers between devices, exchange(): return lax.all_to_all(flat, axis, 0, 0, tiled=True).reshape(array.shape)  13.7 us
    all_to_all x1, starting transfers between devices, exchange(): return lax.all_to_all(flat, axis, 0, 0, tiled=True).reshape(array.shape)  10.6 us
  transfers between devices with their start and end apart: 1, of which 1 were waited for; matrix products, arithmetic and copies ran while one was open for 0% of the time, Pallas kernels for 0%

profile of v1, /device:TPU:8, one launch (start us, length us, event | category | flops | bytes accessed | tf_op | source)
XLA Modules:
  0.0 197.8 jit_solution(70271259202893212)
XLA Ops:
  0.7 0.7 reduce
  1.4 0.1 reshape.93
  1.4 0.5 convert_reduce_fusion
  1.9 0.8 broadcast_in_dim.19
  2.7 0.2 select_reduce_fusion
  2.9 0.1 copy.8
  3.0 0.1 reshape.94.table_ref
  3.1 0.0 copy-start.3
  3.1 0.9 copy-done.3
  4.0 1.5 migrate_pack.1
  5.5 10.6 %all-to-all-start = ((f32[16,48,128]{2,1,0:T(8,128)}), f32[16,48,128]{2,1,0:T(8,128)S(1)}, u32[]{:S(2)}, u32[]{:S(2)}) async-start(f32[16,48,128]{2,1,0:T(8,128)} %bitcast.1), calls=%async_computation | async-start | bytes 786432 | tf_op jit(solution)/shard_map/all_to_all | solution.py:297
  16.0 13.7 %all-to-all-done = f32[16,48,128]{2,1,0:T(8,128)S(1)} async-done(((f32[16,48,128]{2,1,0:T(8,128)}), f32[16,48,128]{2,1,0:T(8,128)S(1)}, u32[]{:S(2)}, u32[]{:S(2)}) %all-to-all-start) | async-done | bytes 393248 | tf_op jit(solution)/shard_map/all_to_all | solution.py:297
  29.7 0.7 copy-done.4
  30.4 0.6 owner_pack.1
  31.0 25.3 %all_to_all.57.in_ref = f32[32,24,128]{2,1,0:T(8,128)S(1)} all-to-all(f32[32,24,128]{2,1,0:T(8,128)S(1)} %owner_pack.1), channel_id=1, replica_groups=mesh['walk'=16,'chol'=32] {'chol'}, dimensions={0} | all-to-all | bytes 786432 | tf_op jit(solution)/shard_map/all_to_all | solution.py:297
  56.3 6.7 %owner_first.1 = (bf16[32,16,128]{2,1,0:T(8,128)(2,1)S(1)}, f32[512,128]{1,0:T(8,128)S(1)}, f32[64,128]{1,0:T(8,128)S(1)}, f32[256,128]{1,0:T(8,128)S(1)}) custom-call(f32[32,24,128]{2,1,0:T(8,128)S(1)} %all_to_all.57.in_ref), custom_call_target="tpu_custom_call" | custom-call | tf_op jit(solution)/shard_map/owner_first/pallas_call | solution.py:279
  63.0 15.0 %all_to_all.58.theta_ref = bf16[32,16,128]{2,1,0:T(8,128)(2,1)S(1)} all-to-all(bf16[32,16,128]{2,1,0:T(8,128)(2,1)S(1)} %get-tuple-element.9), channel_id=1, replica_groups=mesh['walk'=16,'chol'=32] {'chol'}, dimensions={0} | all-to-all | bytes 262144 | tf_op jit(solution)/shard_map/all_to_all | solution.py:297
  78.1 2.0 %copy-done = bf16[896,2048]{1,0:T(8,128)(2,1)S(1)} copy-done((bf16[896,2048]{1,0:T(8,128)(2,1)S(1)}, bf16[896,2048]{1,0:T(8,128)(2,1)}, u32[]{:S(2)}) %copy-start) | copy-done | bytes 3670040
  80.1 0.8 force.2
  80.9 15.6 %all_to_all.59.refs_0_ = bf16[32,32,128]{2,1,0:T(8,128)(2,1)S(1)} all-to-all(bf16[32,32,128]{2,1,0:T(8,128)(2,1)S(1)} %force.2), channel_id=1, replica_groups=mesh['walk'=16,'chol'=32] {'chol'}, dimensions={0} | all-to-all | bytes 524288 | tf_op jit(solution)/shard_map/all_to_all | solution.py:297
  96.6 0.0 copy-done.2
  96.6 0.7 drive.2
  97.3 15.2 %all_to_all.60.drive_ref = bf16[32,32,128]{2,1,0:T(8,128)(2,1)S(1)} all-to-all(bf16[32,32,128]{2,1,0:T(8,128)(2,1)S(1)} %get-tuple-element.10), channel_id=1, replica_groups=mesh['walk'=16,'chol'=32] {'chol'}, dimensions={0} | all-to-all | bytes 524288 | tf_op jit(solution)/shard_map/all_to_all | solution.py:297
  112.5 1.3 push.1
  113.8 15.2 %all_to_all.61.push_ref = f32[32,16,128]{2,1,0:T(8,128)S(1)} all-to-all(f32[32,16,128]{2,1,0:T(8,128)S(1)} %push.1), channel_id=1, replica_groups=mesh['walk'=16,'chol'=32] {'chol'}, dimensions={0} | all-to-all | bytes 524288 | tf_op jit(solution)/shard_map/all_to_all | solution.py:297
  128.9 7.4 %owner_next.1 = bf16[32,112,128]{2,1,0:T(8,128)(2,1)S(1)} custom-call(f32[32,16,128]{2,1,0:T(8,128)S(1)} %all_to_all.61.push_ref, f32[512,128]{1,0:T(8,128)S(1)} %get-tuple-element.11.phi_ref, f32[64,128]{1,0:T(8,128)S(1)} %get-tuple-element.12.corr_ref, f32[256,128]{1,0:T(8,128)S(1)} %get-tuple-element.13.trial_ref), custom_call_target="tpu_custom_call" | custom-call | tf_op jit(solution)/shard_map/owner_next/pallas_call | solution.py:279
  136.3 25.6 %all_to_all.62.theta_ref.bundle_ref = bf16[32,112,128]{2,1,0:T(8,128)(2,1)S(1)} all-to-all(bf16[32,112,128]{2,1,0:T(8,128)(2,1)S(1)} %owner_next.1), channel_id=1, replica_groups=mesh['walk'=16,'chol'=32] {'chol'}, dimensions={0} | all-to-all | bytes 1835008 | tf_op jit(solution)/shard_map/all_to_all | solution.py:297
  161.9 0.8 force.3
  162.7 16.5 %all_to_all.63.refs_0_ = bf16[32,32,128]{2,1,0:T(8,128)(2,1)S(1)} all-to-all(bf16[32,32,128]{2,1,0:T(8,128)(2,1)S(1)} %force.3), channel_id=1, replica_groups=mesh['walk'=16,'chol'=32] {'chol'}, dimensions={0} | all-to-all | bytes 524288 | tf_op jit(solution)/shard_map/all_to_all | solution.py:297
  179.2 0.7 drive.3
  179.9 15.1 %all_to_all.64.drive_ref = bf16[32,32,128]{2,1,0:T(8,128)(2,1)S(1)} all-to-all(bf16[32,32,128]{2,1,0:T(8,128)(2,1)S(1)} %get-tuple-element.14), channel_id=1, replica_groups=mesh['walk'=16,'chol'=32] {'chol'}, dimensions={0} | all-to-all | bytes 524288 | tf_op jit(solution)/shard_map/all_to_all | solution.py:297
  195.0 2.8 %last.1 = f32[48,896]{1,0:T(8,128)} custom-call(bf16[32,32,128]{2,1,0:T(8,128)(2,1)S(1)} %all_to_all.64.drive_ref, bf16[896,2048]{1,0:T(8,128)(2,1)S(1)} %copy-done.1, bf16[32,112,128]{2,1,0:T(8,128)(2,1)S(1)} %all_to_all.62.theta_ref.bundle_ref), custom_call_target="tpu_custom_call" | custom-call | tf_op jit(solution)/shard_map/last/pallas_call | solution.py:279
  (8 shorter events, 0.0 us)
Async XLA Ops:
  3.1 0.9 copy-start.3
  5.5 91.1 %copy-start.2 = (f32[2,48,64]{2,1,0:T(8,128)S(1)}, f32[2,48,64]{2,1,0:T(8,128)}, u32[]{:S(2)}) copy-start(f32[2,48,64]{2,1,0:T(8,128)} %refs_1_.3) | copy-start | bytes 73732
  5.5 24.2 %all-to-all-start = ((f32[16,48,128]{2,1,0:T(8,128)}), f32[16,48,128]{2,1,0:T(8,128)S(1)}, u32[]{:S(2)}, u32[]{:S(2)}) async-start(f32[16,48,128]{2,1,0:T(8,128)} %bitcast.1), calls=%async_computation | async-start | bytes 786432 | tf_op jit(solution)/shard_map/all_to_all | solution.py:297
  29.7 0.7 copy-start.4
  78.1 2.0 %copy-start = (bf16[896,2048]{1,0:T(8,128)(2,1)S(1)}, bf16[896,2048]{1,0:T(8,128)(2,1)}, u32[]{:S(2)}) copy-start(bf16[896,2048]{1,0:T(8,128)(2,1)} %lrot_ref.7) | copy-start | bytes 11010052
  80.1 32.4 %copy-start.1 = (bf16[896,2048]{1,0:T(8,128)(2,1)S(1)}, bf16[896,2048]{1,0:T(8,128)(2,1)}, u32[]{:S(2)}) copy-start(bf16[896,2048]{1,0:T(8,128)(2,1)} %lrot_ref.7) | copy-start | bytes 11010052

commit v2 on v1

--- a/solution.py
+++ b/solution.py
@@ -16,6 +16,7 @@
 WALKERS = 48
 OWNERS = 24
 CAP = 6
+PANEL = 8
 CHOLS = 2048
 TAU = 0.03
 EXACT = lax.Precision.HIGHEST
@@ -86,16 +87,19 @@
     lanes = lane_ids(ELECS)
     row_ids = lax.broadcasted_iota(jnp.int32, (ELECS, LANES), 0)
     within = lanes & (HALF - 1)
-    for k in range(ELECS):
-        column = jnp.where(
-            lanes < HALF,
-            jnp.broadcast_to(gram[:, k:k + 1], (ELECS, LANES)),
-            jnp.broadcast_to(gram[:, HALF + k:HALF + k + 1], (ELECS, LANES)),
-        )
-        pivot = column[k:k + 1, :]
-        row = jnp.where(within[k:k + 1, :] == k, 1.0, gram[k:k + 1, :]) / pivot
-        gram = jnp.where(within == k, 0.0, gram) - column * row
-        gram = jnp.where(row_ids == k, jnp.broadcast_to(row, (ELECS, LANES)), gram)
+    base = lanes & HALF
+    for start in range(0, ELECS, PANEL):
+        columns = {
+            m: jnp.take_along_axis(gram, base + m, axis=1) for m in range(start, start + PANEL)
+        }
+        for k in range(start, start + PANEL):
+            column = columns.pop(k)
+            scale = 1.0 / column[k:k + 1, :]
+            row = jnp.where(within[0:1] == k, 1.0, gram[k:k + 1, :]) * scale
+            for m in columns:
+                entry = columns[m][k:k + 1, :] * scale
+                columns[m] = jnp.where(row_ids == k, entry, columns[m] - column * entry)
+            gram = jnp.where(row_ids == k, row, jnp.where(within == k, 0.0, gram) - column * row)
     return gram
 
 
@@ -117,12 +121,29 @@
     return [theta[DEVS * a:DEVS * (a + 1)] for a in range(ORBS)]
 
 
-def migrate_pack(table_ref, phi_ref, out_ref, rows_ref):
+def migrate_pack(group_ref, source_ref, slot_ref, phi_ref, out_ref):
+    count = source_ref.shape[1]
+    groups = count // WALKERS
+    cap = out_ref.shape[0] // groups
+    walker = lax.broadcasted_iota(jnp.int32, (8, count), 1)
+    block = lax.div(walker, WALKERS)
+    place = walker - block * WALKERS
+    mine = jnp.broadcast_to((source_ref[...] == group_ref[0]).astype(jnp.int32), (8, count))
+    order = mine
+    step = 1
+    while step < WALKERS:
+        order = order + jnp.where(place >= step, pltpu.roll(order, step, 1), 0)
+        step *= 2
+    target = jnp.where(mine == 1, block * cap + order - 1, -1)[0:1]
+    row_ids = lax.broadcasted_iota(jnp.int32, (groups * cap, count), 0)
+    slot_ids = lax.broadcasted_iota(jnp.int32, (WALKERS, count), 0)
+    taken = jnp.where(row_ids == target, 1.0, 0.0).astype(BF16)
+    held = jnp.where(slot_ids == slot_ref[...], 1.0, 0.0).astype(BF16)
+    choice = lax.dot_general(taken, held, (((1,), (1,)), ((), ())), preferred_element_type=F32)
+    rows = exact_dot(choice, phi_ref[...], 1, 0)
     for tile in range(TILES):
-        rows_ref[:, tile, :] = phi_ref[:, tile * LANES:(tile + 1) * LANES]
-    rows_ref[:, TILES, :] = jnp.zeros((WALKERS, LANES), F32)
-    for j in range(out_ref.shape[0]):
-        out_ref[j] = rows_ref[table_ref[j]]
+        out_ref[:, tile, :] = rows[:, tile * LANES:(tile + 1) * LANES]
+    out_ref[:, TILES, :] = jnp.zeros((groups * cap, LANES), F32)
 
 
 def owner_pack(place_ref, rows_ref, trial_ref, out_ref, pad_ref):
@@ -138,13 +159,13 @@
         out_ref[d, 16:24, :] = trial
 
 
-def store_theta(theta, wide_ref, out_ref):
+def store_walkers(blocks, first, wide_ref, out_ref):
     lanes = lane_ids(DEVS)
     for half in range(2):
         for tile in range(TILES):
-            wide_ref[:, 8 * half + tile, :] = unpack_tile(theta, tile, half, lanes)
+            wide_ref[:, 8 * half + tile, :] = unpack_tile(blocks, tile, half, lanes)
         wide_ref[:, 8 * half + TILES, :] = jnp.zeros((DEVS, LANES), F32)
-    out_ref[:, 0:16, :] = wide_ref[...].astype(BF16)
+    out_ref[:, first:first + 16, :] = wide_ref[...].astype(BF16)
 
 
 def owner_first(in_ref, theta_ref, phi_ref, corr_ref, trial_ref, wide_ref):
@@ -156,28 +177,23 @@
     phi_ref[...] = walkers
     corr_ref[...] = correlation
     trial_ref[...] = trial
-    store_theta(theta_blocks(walkers, correlation), wide_ref, theta_ref)
+    store_walkers(theta_blocks(walkers, correlation), 0, wide_ref, theta_ref)
 
 
 def owner_next(push_ref, phi_ref, corr_ref, trial_ref, out_ref, wide_ref):
     lanes = lane_ids(DEVS)
-    tiles = [[push_ref[:, 8 * h + k, :] for k in range(TILES)] for h in range(2)]
+    wide_ref[...] = push_ref[...].astype(F32)
+    tiles = [[wide_ref[:, 8 * h + k, :] for k in range(TILES)] for h in range(2)]
     push = jnp.concatenate(pack_pair(tiles[0], tiles[1], lanes), axis=0)
     old = block_diagonal(corr_ref[...], lane_ids(HALF))
     walkers = phi_ref[...] + TAU * exact_dot(push, old, 1, 0)
     correlation = correlate(trial_ref[...], walkers)
-    theta = theta_blocks(walkers, correlation)
-    store_theta(theta, wide_ref, out_ref)
+    store_walkers(theta_blocks(walkers, correlation), 0, wide_ref, out_ref)
     blocks = [walkers[DEVS * a:DEVS * (a + 1)] for a in range(ORBS)]
-    for half in range(2):
-        for tile in range(TILES):
-            wide_ref[:, 8 * half + tile, :] = unpack_tile(blocks, tile, half, lanes)
-    high = wide_ref[...].astype(BF16)
-    out_ref[:, 16:32, :] = high
-    out_ref[:, 32:48, :] = (wide_ref[...] - high.astype(F32)).astype(BF16)
+    store_walkers(blocks, 16, wide_ref, out_ref)
     sent = correlation.astype(BF16)
     for d in range(DEVS):
-        out_ref[d, 48:112, :] = sent
+        out_ref[d, 32:96, :] = sent
 
 
 def force_kernel(theta_ref, lrot_ref, out_ref, wide_ref):
@@ -190,11 +206,10 @@
         axis=0,
     ).astype(BF16)
     force = jnp.dot(theta, lrot_ref[...], preferred_element_type=F32)
-    force = jnp.concatenate([force, jnp.zeros((16, CHOLS), F32)], axis=0)
-    lanes = lane_ids(32)
+    lanes = lane_ids(OWNERS)
     for pair in range(DEVS // 2):
         block = force[:, pair * LANES:(pair + 1) * LANES]
-        top, low = block[:32], block[32:]
+        top, low = block[:OWNERS], block[OWNERS:]
         out_ref[2 * pair] = jnp.where(lanes < HALF, top, turn(low, HALF)).astype(BF16)
         out_ref[2 * pair + 1] = jnp.where(lanes < HALF, turn(top, HALF), low).astype(BF16)
 
@@ -205,24 +220,24 @@
         total = total + force_ref[c].astype(F32)
     capped = jnp.clip(20.0 * total, -1.0, 1.0)
     pad_ref[...] = jnp.zeros_like(pad_ref)
-    pad_ref[0:WALKERS, 0:HALF] = fields_ref[step]
-    lanes = lane_ids(32)
-    fields = jnp.where(lanes < HALF, pad_ref[0:32, :], turn(pad_ref[32:64, :], HALF))
+    pad_ref[:, 0:HALF] = fields_ref[step]
+    lanes = lane_ids(OWNERS)
+    fields = jnp.where(lanes < HALF, pad_ref[0:OWNERS, :], turn(pad_ref[OWNERS:, :], HALF))
     drive = (fields - capped).astype(BF16)
     for d in range(DEVS):
         out_ref[d] = drive
-    capped_ref[0:32, :] = capped[:, 0:HALF]
-    capped_ref[32:WALKERS, :] = turn(capped, HALF)[0:WALKERS - 32, 0:HALF]
+    capped_ref[0:OWNERS, :] = capped[:, 0:HALF]
+    capped_ref[OWNERS:, :] = turn(capped, HALF)[:, 0:HALF]
 
 
 def gather_push(drive_ref, lrot_ref):
-    lanes = lane_ids(32)
+    lanes = lane_ids(OWNERS)
     tops, lows = [], []
     for pair in range(DEVS // 2):
         left = drive_ref[2 * pair].astype(F32)
         right = drive_ref[2 * pair + 1].astype(F32)
         tops.append(jnp.where(lanes < HALF, left, turn(right, HALF)))
-        lows.append(jnp.where(lanes < HALF, turn(left, HALF), right)[0:16])
+        lows.append(jnp.where(lanes < HALF, turn(left, HALF), right))
     drive = jnp.concatenate(
         [jnp.concatenate(tops, axis=1), jnp.concatenate(lows, axis=1)], axis=0
     ).astype(BF16)
@@ -231,14 +246,15 @@
     )
 
 
-def push_kernel(drive_ref, lrot_ref, out_ref):
+def push_kernel(drive_ref, lrot_ref, out_ref, wide_ref):
     push = gather_push(drive_ref, lrot_ref)
     for half in range(2):
         rows = push[OWNERS * half:OWNERS * (half + 1)]
         for tile in range(TILES):
-            out_ref[0:OWNERS, 8 * half + tile, :] = rows[:, tile * LANES:(tile + 1) * LANES]
-        out_ref[0:OWNERS, 8 * half + TILES, :] = jnp.zeros((OWNERS, LANES), F32)
-    out_ref[OWNERS:, :, :] = jnp.zeros((DEVS - OWNERS, 16, LANES), F32)
+            wide_ref[:, 8 * half + tile, :] = rows[:, tile * LANES:(tile + 1) * LANES]
+        wide_ref[:, 8 * half + TILES, :] = jnp.zeros((OWNERS, LANES), F32)
+    out_ref[0:OWNERS] = wide_ref[...].astype(BF16)
+    out_ref[OWNERS:] = jnp.zeros((DEVS - OWNERS, 16, LANES), BF16)
 
 
 def last_kernel(drive_ref, lrot_ref, bundle_ref, out_ref, push_ref, wide_ref):
@@ -256,7 +272,7 @@
         push_ref[:, orbital, :] = blocks[orbital]
     square = lane_ids(HALF)
     for d in range(OWNERS):
-        pair = block_diagonal(bundle_ref[d, 48:112, :].astype(F32), square).astype(BF16)
+        pair = block_diagonal(bundle_ref[d, 32:96, :].astype(F32), square).astype(BF16)
         rows = push_ref[d]
         high = rows.astype(BF16)
         low = (rows - high.astype(F32)).astype(BF16)
@@ -265,7 +281,7 @@
             + jnp.dot(low, pair, preferred_element_type=F32)
         )
     moved = [push_ref[:, orbital, :] for orbital in range(ORBS)]
-    wide_ref[...] = bundle_ref[0:OWNERS, 16:32, :].astype(F32) + bundle_ref[0:OWNERS, 32:48, :].astype(F32)
+    wide_ref[...] = bundle_ref[0:OWNERS, 16:32, :].astype(F32)
     for half in range(2):
         for tile in range(TILES):
             out_ref[OWNERS * half:OWNERS * (half + 1), tile * LANES:(tile + 1) * LANES] = (
@@ -273,7 +289,7 @@
             )
 
 
-def call(kernel, name, shapes, operands, in_specs, scratch=(), limit=48):
+def call(kernel, name, shapes, operands, in_specs, scratch=(), limit=24, micros=1.0):
     single = not isinstance(shapes, (list, tuple))
     listed = [shapes] if single else list(shapes)
     result = pl.pallas_call(
@@ -283,6 +299,7 @@
         out_specs=vmem(len(listed)),
         scratch_shapes=list(scratch),
         compiler_params=pltpu.CompilerParams(vmem_limit_bytes=limit * 1024 * 1024),
+        cost_estimate=pl.CostEstimate(flops=int(micros * 1e9), bytes_accessed=0, transcendentals=0),
         name=name,
     )(*operands)
     return result[0] if single else result
@@ -297,27 +314,21 @@
     return lax.all_to_all(flat, axis, 0, 0, tiled=True).reshape(array.shape)
 
 
-def tables(src_group, src_slot, groups, own_group, cap):
-    source = src_group.reshape(groups, WALKERS)
-    slots = src_slot.reshape(groups, WALKERS)
+def places(src_group, own_group, cap):
+    source = lax.dynamic_slice_in_dim(src_group.reshape(-1), own_group * WALKERS, WALKERS)
     order = jnp.arange(WALKERS, dtype=jnp.int32)
-    earlier = (source[:, None, :] == source[:, :, None]) & (order[None, None, :] < order[None, :, None])
-    rank = jnp.sum(earlier.astype(jnp.int32), axis=2)
-    picked = (source == own_group)[:, None, :] & (
-        rank[:, None, :] == jnp.arange(cap, dtype=jnp.int32)[None, :, None]
-    )
-    send = jnp.sum(jnp.where(picked, slots[:, None, :], 0), axis=2).reshape(groups * cap)
-    own_source = lax.dynamic_index_in_dim(source, own_group, 0, keepdims=False)
-    own_rank = lax.dynamic_index_in_dim(rank, own_group, 0, keepdims=False)
-    return send.astype(jnp.int32), (own_source * cap + own_rank).astype(jnp.int32)
+    earlier = (source[None, :] == source[:, None]) & (order[None, :] < order[:, None])
+    return source * cap + jnp.sum(earlier.astype(jnp.int32), axis=1)
 
 
 def body(phi_in, trial, lrot, fields, src_group, src_slot, cap=CAP):
     groups = lax.axis_size("walk")
-    send, place = tables(src_group, src_slot, groups, lax.axis_index("walk"), cap)
+    own_group = lax.axis_index("walk")
+    place = places(src_group, own_group, cap)
     rows = call(
-        migrate_pack, "migrate_pack", shape((groups * cap, 8, LANES)), (send, phi_in),
-        smem() + vmem(), [pltpu.VMEM((WALKERS, 8, LANES), F32)],
+        migrate_pack, "migrate_pack", shape((groups * cap, 8, LANES)),
+        (own_group.reshape(1), src_group.reshape(1, -1), src_slot.reshape(1, -1), phi_in),
+        smem() + vmem(3),
     )
     rows = exchange(rows, "walk")
     owned = call(
@@ -333,28 +344,28 @@
             shape((DEVS, 16, LANES), BF16), shape((DEVS * ORBS, LANES)),
             shape((HALF, LANES)), shape((DEVS * ORBS // 2, LANES)),
         ],
-        (owned,), vmem(), [wide],
+        (owned,), vmem(), [wide], micros=6.0,
     )
     theta = exchange(theta, "chol")
 
     def forces(theta, step):
         force = call(
-            force_kernel, "force", shape((DEVS, 32, LANES), BF16), (theta, lrot), vmem(2), [few]
+            force_kernel, "force", shape((DEVS, OWNERS, LANES), BF16), (theta, lrot), vmem(2), [few]
         )
         force = exchange(force, "chol")
         drive, capped = call(
             lambda *refs: drive_kernel(step, *refs), "drive",
-            [shape((DEVS, 32, LANES), BF16), shape((WALKERS, HALF))],
-            (force, fields), vmem(2), [pltpu.VMEM((64, LANES), F32)],
+            [shape((DEVS, OWNERS, LANES), BF16), shape((WALKERS, HALF))],
+            (force, fields), vmem(2), [pltpu.VMEM((WALKERS, LANES), F32)],
         )
         return exchange(drive, "chol"), capped
 
     drive, _ = forces(theta, 0)
-    push = call(push_kernel, "push", shape((DEVS, 16, LANES)), (drive, lrot), vmem(2))
+    push = call(push_kernel, "push", shape((DEVS, 16, LANES), BF16), (drive, lrot), vmem(2), [few])
     push = exchange(push, "chol")
     bundle = call(
-        owner_next, "owner_next", shape((DEVS, 112, LANES), BF16),
-        (push, phi, corr, trial_all), vmem(4), [wide],
+        owner_next, "owner_next", shape((DEVS, 96, LANES), BF16),
+        (push, phi, corr, trial_all), vmem(4), [wide], micros=6.0,
     )
     bundle = exchange(bundle, "chol")
     drive, capped = forces(bundle, 1)

time: 198 us -> 181 us (0.914)
  blocking collectives: 143 us -> 136 us
  Pallas kernels: 23.4 us -> 17.4 us
    all_to_all x8, blocking collectives: 143 us -> 136 us  [exchange(): return lax.all_to_all(flat, axis, 0, 0, tiled=True).reshape(array.shape)]
    pallas_call x10, Pallas kernels: 23.4 us -> 17.4 us  [call(): pl.pallas_call(kernel, out_shape=listed, in_specs=in_specs, out_specs=vme...]
    unnamed x10, local copies, waits for them, and re-layouts: 3.66 us -> 1.62 us
  transfers between devices with their start and end apart: 1 -> 1, of which waited for: 1 -> 1; matrix products, arithmetic and copies ran while one was open for 0% -> 1% of each run, Pallas kernels for 0% -> 0%
where the time goes in v2:
time: 181 us; the launch traced here: 180 us
  blocking collectives  136 us (75%)
  Pallas kernels  17.4 us (10%)
  waiting for transfers between devices  12 us (7%)
  starting transfers between devices  10.4 us (6%)
  local copies, waits for them, and re-layouts  3.07 us (2%)
    all_to_all x8, blocking collectives, exchange(): return lax.all_to_all(flat, axis, 0, 0, tiled=True).reshape(array.shape)  136 us
    pallas_call x10, Pallas kernels, call(): pl.pallas_call(kernel, out_shape=listed, in_specs=in_specs, out_specs=vme...  17.4 us
    all_to_all x1, waiting for transfers between devices, exchange(): return lax.all_to_all(flat, axis, 0, 0, tiled=True).reshape(array.shape)  12 us
    all_to_all x1, starting transfers between devices, exchange(): return lax.all_to_all(flat, axis, 0, 0, tiled=True).reshape(array.shape)  10.4 us
  transfers between devices with their start and end apart: 1, of which 1 were waited for; matrix products, arithmetic and copies ran while one was open for 1% of the time, Pallas kernels for 0%

profile of v2, /device:TPU:8, one launch (start us, length us, event | category | flops | bytes accessed | tf_op | source)
XLA Modules:
  0.0 180.1 jit_solution(7544282128144697124)
XLA Ops:
  0.6 0.0 copy-start.4
  0.6 0.7 reshape.76.slot_ref
  1.3 0.7 copy-done.1
  2.0 0.0 copy-start.2
  2.0 0.9 copy-done.2
  2.9 1.8 %migrate_pack.1 = f32[96,8,128]{2,1,0:T(8,128)} custom-call(s32[1]{0:T(128)} %bitcast.1.group_ref, s32[1,768]{1,0:T(1,128)S(1)} %bitcast.9, s32[1,768]{1,0:T(1,128)S(1)} %reshape.76.slot_ref, f32[48,896]{1,0:T(8,128)S(1)} %copy-done.2), custom_call_target="tpu_custom_call" | custom-call | flops 1000000000 | tf_op jit(solution)/shard_map/migrate_pack/pallas_call | solution.py:295
  4.8 10.4 %all-to-all-start = ((f32[16,48,128]{2,1,0:T(8,128)}), f32[16,48,128]{2,1,0:T(8,128)S(1)}, u32[]{:S(2)}, u32[]{:S(2)}) async-start(f32[16,48,128]{2,1,0:T(8,128)} %bitcast.3), calls=%async_computation | async-start | bytes 786432 | tf_op jit(solution)/shard_map/all_to_all | solution.py:314
  15.2 0.8 dynamic-slice_bitcast_fusion
  16.0 0.2 convert_reduce_fusion
  16.1 0.8 multiply_add_fusion.place_ref
  16.9 12.0 %all-to-all-done = f32[16,48,128]{2,1,0:T(8,128)S(1)} async-done(((f32[16,48,128]{2,1,0:T(8,128)}), f32[16,48,128]{2,1,0:T(8,128)S(1)}, u32[]{:S(2)}, u32[]{:S(2)}) %all-to-all-start) | async-done | bytes 393248 | tf_op jit(solution)/shard_map/all_to_all | solution.py:314
  28.9 0.0 copy-done.4
  28.9 0.6 owner_pack.1
  29.5 25.3 %all_to_all.57.in_ref = f32[32,24,128]{2,1,0:T(8,128)S(1)} all-to-all(f32[32,24,128]{2,1,0:T(8,128)S(1)} %owner_pack.1), channel_id=1, replica_groups=mesh['walk'=16,'chol'=32] {'chol'}, dimensions={0} | all-to-all | bytes 786432 | tf_op jit(solution)/shard_map/all_to_all | solution.py:314
  54.8 3.6 %owner_first.1 = (bf16[32,16,128]{2,1,0:T(8,128)(2,1)S(1)}, f32[512,128]{1,0:T(8,128)S(1)}, f32[64,128]{1,0:T(8,128)S(1)}, f32[256,128]{1,0:T(8,128)S(1)}) custom-call(f32[32,24,128]{2,1,0:T(8,128)S(1)} %all_to_all.57.in_ref), custom_call_target="tpu_custom_call" | custom-call | flops 6000000000 | tf_op jit(solution)/shard_map/owner_first/pallas_call | solution.py:295
  58.4 0.0 copy-start.3
  58.4 15.2 %all_to_all.58.theta_ref = bf16[32,16,128]{2,1,0:T(8,128)(2,1)S(1)} all-to-all(bf16[32,16,128]{2,1,0:T(8,128)(2,1)S(1)} %get-tuple-element.9), channel_id=1, replica_groups=mesh['walk'=16,'chol'=32] {'chol'}, dimensions={0} | all-to-all | bytes 262144 | tf_op jit(solution)/shard_map/all_to_all | solution.py:314
  73.6 0.0 copy-done
  73.6 0.8 force.2
  74.4 14.3 %all_to_all.59.refs_0_ = bf16[32,24,128]{2,1,0:T(8,128)(2,1)S(1)} all-to-all(bf16[32,24,128]{2,1,0:T(8,128)(2,1)S(1)} %force.2), channel_id=1, replica_groups=mesh['walk'=16,'chol'=32] {'chol'}, dimensions={0} | all-to-all | bytes 393216 | tf_op jit(solution)/shard_map/all_to_all | solution.py:314
  88.7 0.0 copy-done.3
  88.7 0.7 drive.2
  89.4 14.4 %all_to_all.60.drive_ref = bf16[32,24,128]{2,1,0:T(8,128)(2,1)S(1)} all-to-all(bf16[32,24,128]{2,1,0:T(8,128)(2,1)S(1)} %get-tuple-element.10), channel_id=1, replica_groups=mesh['walk'=16,'chol'=32] {'chol'}, dimensions={0} | all-to-all | bytes 393216 | tf_op jit(solution)/shard_map/all_to_all | solution.py:314
  103.8 1.3 push.1
  105.1 13.9 %all_to_all.61.push_ref = bf16[32,16,128]{2,1,0:T(8,128)(2,1)S(1)} all-to-all(bf16[32,16,128]{2,1,0:T(8,128)(2,1)S(1)} %push.1), channel_id=1, replica_groups=mesh['walk'=16,'chol'=32] {'chol'}, dimensions={0} | all-to-all | bytes 262144 | tf_op jit(solution)/shard_map/all_to_all | solution.py:314
  118.9 4.2 %owner_next.1 = bf16[32,96,128]{2,1,0:T(8,128)(2,1)S(1)} custom-call(bf16[32,16,128]{2,1,0:T(8,128)(2,1)S(1)} %all_to_all.61.push_ref, f32[512,128]{1,0:T(8,128)S(1)} %get-tuple-element.11.phi_ref, f32[64,128]{1,0:T(8,128)S(1)} %get-tuple-element.12.corr_ref, f32[256,128]{1,0:T(8,128)S(1)} %get-tuple-element.13.trial_ref), custom_call_target="tpu_custom_call" | custom-call | flops 6000000000 | tf_op jit(solution)/shard_map/owner_next/pallas_call | solution.py:295
  123.2 22.5 %all_to_all.62.theta_ref.bundle_ref = bf16[32,96,128]{2,1,0:T(8,128)(2,1)S(1)} all-to-all(bf16[32,96,128]{2,1,0:T(8,128)(2,1)S(1)} %owner_next.1), channel_id=1, replica_groups=mesh['walk'=16,'chol'=32] {'chol'}, dimensions={0} | all-to-all | bytes 1572864 | tf_op jit(solution)/shard_map/all_to_all | solution.py:314
  145.6 0.8 force.3
  146.4 15.6 %all_to_all.63.refs_0_ = bf16[32,24,128]{2,1,0:T(8,128)(2,1)S(1)} all-to-all(bf16[32,24,128]{2,1,0:T(8,128)(2,1)S(1)} %force.3), channel_id=1, replica_groups=mesh['walk'=16,'chol'=32] {'chol'}, dimensions={0} | all-to-all | bytes 393216 | tf_op jit(solution)/shard_map/all_to_all | solution.py:314
  162.1 0.7 drive.3
  162.8 14.5 %all_to_all.64.drive_ref = bf16[32,24,128]{2,1,0:T(8,128)(2,1)S(1)} all-to-all(bf16[32,24,128]{2,1,0:T(8,128)(2,1)S(1)} %get-tuple-element.14), channel_id=1, replica_groups=mesh['walk'=16,'chol'=32] {'chol'}, dimensions={0} | all-to-all | bytes 393216 | tf_op jit(solution)/shard_map/all_to_all | solution.py:314
  177.2 2.8 %last.1 = f32[48,896]{1,0:T(8,128)} custom-call(bf16[32,24,128]{2,1,0:T(8,128)(2,1)S(1)} %all_to_all.64.drive_ref, bf16[896,2048]{1,0:T(8,128)(2,1)S(1)} %copy-done, bf16[32,96,128]{2,1,0:T(8,128)(2,1)S(1)} %all_to_all.62.theta_ref.bundle_ref), custom_call_target="tpu_custom_call" | custom-call | flops 1000000000 | tf_op jit(solution)/shard_map/last/pallas_call | solution.py:295
  (2 shorter events, 0.0 us)
Async XLA Ops:
  0.6 28.3 %copy-start.4 = (f32[16,56]{1,0:T(8,128)S(1)}, f32[16,56]{1,0:T(8,128)}, u32[]{:S(2)}) copy-start(f32[16,56]{1,0:T(8,128)} %trial_ref.1) | copy-start | bytes 10756
  1.3 0.7 copy-start.1
  2.0 0.9 copy-start.2
  4.8 24.1 %all-to-all-start = ((f32[16,48,128]{2,1,0:T(8,128)}), f32[16,48,128]{2,1,0:T(8,128)S(1)}, u32[]{:S(2)}, u32[]{:S(2)}) async-start(f32[16,48,128]{2,1,0:T(8,128)} %bitcast.3), calls=%async_computation | async-start | bytes 786432 | tf_op jit(solution)/shard_map/all_to_all | solution.py:314
  54.8 18.7 %copy-start = (bf16[896,2048]{1,0:T(8,128)(2,1)S(1)}, bf16[896,2048]{1,0:T(8,128)(2,1)}, u32[]{:S(2)}) copy-start(bf16[896,2048]{1,0:T(8,128)(2,1)} %lrot_ref.7) | copy-start | bytes 11010052
  58.4 30.3 %copy-start.3 = (f32[2,48,64]{2,1,0:T(8,128)S(1)}, f32[2,48,64]{2,1,0:T(8,128)}, u32[]{:S(2)}) copy-start(f32[2,48,64]{2,1,0:T(8,128)} %refs_1_.3) | copy-start | bytes 73732

commit v3 on v2

--- a/solution.py
+++ b/solution.py
@@ -121,7 +121,14 @@
     return [theta[DEVS * a:DEVS * (a + 1)] for a in range(ORBS)]
 
 
-def migrate_pack(group_ref, source_ref, slot_ref, phi_ref, out_ref):
+def migrate_pack(
+    group_ref, source_hbm, slot_hbm, phi_hbm, out_ref, source_ref, slot_ref, phi_ref, sems
+):
+    pairs = ((source_hbm, source_ref), (slot_hbm, slot_ref), (phi_hbm, phi_ref))
+    copies = [pltpu.make_async_copy(a, b, sems.at[i]) for i, (a, b) in enumerate(pairs)]
+    for copy in copies:
+        copy.start()
+    copies[0].wait()
     count = source_ref.shape[1]
     groups = count // WALKERS
     cap = out_ref.shape[0] // groups
@@ -138,8 +145,10 @@
     row_ids = lax.broadcasted_iota(jnp.int32, (groups * cap, count), 0)
     slot_ids = lax.broadcasted_iota(jnp.int32, (WALKERS, count), 0)
     taken = jnp.where(row_ids == target, 1.0, 0.0).astype(BF16)
-    held = jnp.where(slot_ids == slot_ref[...], 1.0, 0.0).astype(BF16)
+    copies[1].wait()
+    held = jnp.where(slot_ids == slot_ref[...].reshape(1, count), 1.0, 0.0).astype(BF16)
     choice = lax.dot_general(taken, held, (((1,), (1,)), ((), ())), preferred_element_type=F32)
+    copies[2].wait()
     rows = exact_dot(choice, phi_ref[...], 1, 0)
     for tile in range(TILES):
         out_ref[:, tile, :] = rows[:, tile * LANES:(tile + 1) * LANES]
@@ -159,13 +168,13 @@
         out_ref[d, 16:24, :] = trial
 
 
-def store_walkers(blocks, first, wide_ref, out_ref):
+def store_walkers(blocks, wide_ref, out_ref):
     lanes = lane_ids(DEVS)
     for half in range(2):
         for tile in range(TILES):
             wide_ref[:, 8 * half + tile, :] = unpack_tile(blocks, tile, half, lanes)
         wide_ref[:, 8 * half + TILES, :] = jnp.zeros((DEVS, LANES), F32)
-    out_ref[:, first:first + 16, :] = wide_ref[...].astype(BF16)
+    out_ref[:, 0:16, :] = wide_ref[...].astype(BF16)
 
 
 def owner_first(in_ref, theta_ref, phi_ref, corr_ref, trial_ref, wide_ref):
@@ -177,10 +186,10 @@
     phi_ref[...] = walkers
     corr_ref[...] = correlation
     trial_ref[...] = trial
-    store_walkers(theta_blocks(walkers, correlation), 0, wide_ref, theta_ref)
-
-
-def owner_next(push_ref, phi_ref, corr_ref, trial_ref, out_ref, wide_ref):
+    store_walkers(theta_blocks(walkers, correlation), wide_ref, theta_ref)
+
+
+def owner_next(push_ref, phi_ref, corr_ref, trial_ref, out_ref, next_phi_ref, next_corr_ref, wide_ref):
     lanes = lane_ids(DEVS)
     wide_ref[...] = push_ref[...].astype(F32)
     tiles = [[wide_ref[:, 8 * h + k, :] for k in range(TILES)] for h in range(2)]
@@ -188,15 +197,22 @@
     old = block_diagonal(corr_ref[...], lane_ids(HALF))
     walkers = phi_ref[...] + TAU * exact_dot(push, old, 1, 0)
     correlation = correlate(trial_ref[...], walkers)
-    store_walkers(theta_blocks(walkers, correlation), 0, wide_ref, out_ref)
-    blocks = [walkers[DEVS * a:DEVS * (a + 1)] for a in range(ORBS)]
-    store_walkers(blocks, 16, wide_ref, out_ref)
-    sent = correlation.astype(BF16)
+    next_phi_ref[...] = walkers
+    next_corr_ref[...] = correlation
+    store_walkers(theta_blocks(walkers, correlation), wide_ref, out_ref)
+    sent = correlation[0:32].astype(BF16)
     for d in range(DEVS):
-        out_ref[d, 32:96, :] = sent
-
-
-def force_kernel(theta_ref, lrot_ref, out_ref, wide_ref):
+        out_ref[d, 16:48, :] = sent
+
+
+def phi_pack(phi_ref, out_ref, wide_ref):
+    blocks = [phi_ref[DEVS * a:DEVS * (a + 1), :] for a in range(ORBS)]
+    store_walkers(blocks, wide_ref, out_ref)
+
+
+def force_kernel(theta_ref, lrot_ref, *refs):
+    *rest_ref, out_ref, wide_ref = refs
+    rest = [ref[32:ELECS, :] for ref in rest_ref]
     wide_ref[...] = theta_ref[0:OWNERS, 0:16, :].astype(F32)
     theta = jnp.concatenate(
         [
@@ -210,22 +226,26 @@
     for pair in range(DEVS // 2):
         block = force[:, pair * LANES:(pair + 1) * LANES]
         top, low = block[:OWNERS], block[OWNERS:]
-        out_ref[2 * pair] = jnp.where(lanes < HALF, top, turn(low, HALF)).astype(BF16)
-        out_ref[2 * pair + 1] = jnp.where(lanes < HALF, turn(top, HALF), low).astype(BF16)
-
-
-def drive_kernel(step, force_ref, fields_ref, out_ref, capped_ref, pad_ref):
+        even = jnp.where(lanes < HALF, top, turn(low, HALF))
+        odd = jnp.where(lanes < HALF, turn(top, HALF), low)
+        out_ref[2 * pair] = jnp.concatenate([even] + rest, axis=0).astype(BF16)
+        out_ref[2 * pair + 1] = jnp.concatenate([odd] + rest, axis=0).astype(BF16)
+
+
+def drive_kernel(step, force_ref, fields_ref, *refs):
+    *rest_ref, out_ref, capped_ref, pad_ref = refs
     total = force_ref[0].astype(F32)
     for c in range(1, DEVS):
         total = total + force_ref[c].astype(F32)
-    capped = jnp.clip(20.0 * total, -1.0, 1.0)
+    capped = jnp.clip(20.0 * total[0:OWNERS], -1.0, 1.0)
     pad_ref[...] = jnp.zeros_like(pad_ref)
     pad_ref[:, 0:HALF] = fields_ref[step]
     lanes = lane_ids(OWNERS)
     fields = jnp.where(lanes < HALF, pad_ref[0:OWNERS, :], turn(pad_ref[OWNERS:, :], HALF))
-    drive = (fields - capped).astype(BF16)
+    drive = fields - capped
     for d in range(DEVS):
-        out_ref[d] = drive
+        rest = [ref[d].astype(F32) for ref in rest_ref]
+        out_ref[d] = jnp.concatenate([drive] + rest, axis=0).astype(BF16)
     capped_ref[0:OWNERS, :] = capped[:, 0:HALF]
     capped_ref[OWNERS:, :] = turn(capped, HALF)[:, 0:HALF]
 
@@ -234,8 +254,8 @@
     lanes = lane_ids(OWNERS)
     tops, lows = [], []
     for pair in range(DEVS // 2):
-        left = drive_ref[2 * pair].astype(F32)
-        right = drive_ref[2 * pair + 1].astype(F32)
+        left = drive_ref[2 * pair].astype(F32)[0:OWNERS]
+        right = drive_ref[2 * pair + 1].astype(F32)[0:OWNERS]
         tops.append(jnp.where(lanes < HALF, left, turn(right, HALF)))
         lows.append(jnp.where(lanes < HALF, turn(left, HALF), right))
     drive = jnp.concatenate(
@@ -257,7 +277,7 @@
     out_ref[OWNERS:] = jnp.zeros((DEVS - OWNERS, 16, LANES), BF16)
 
 
-def last_kernel(drive_ref, lrot_ref, bundle_ref, out_ref, push_ref, wide_ref):
+def last_kernel(drive_ref, lrot_ref, theta_ref, force_ref, out_ref, push_ref, wide_ref):
     push = gather_push(drive_ref, lrot_ref)
     lanes = lane_ids(OWNERS)
     tiles = [
@@ -272,16 +292,19 @@
         push_ref[:, orbital, :] = blocks[orbital]
     square = lane_ids(HALF)
     for d in range(OWNERS):
-        pair = block_diagonal(bundle_ref[d, 32:96, :].astype(F32), square).astype(BF16)
-        rows = push_ref[d]
-        high = rows.astype(BF16)
-        low = (rows - high.astype(F32)).astype(BF16)
-        push_ref[d] = TAU * (
-            jnp.dot(high, pair, preferred_element_type=F32)
-            + jnp.dot(low, pair, preferred_element_type=F32)
+        pair = jnp.concatenate(
+            [
+                theta_ref[d, 16:48, :].astype(F32),
+                force_ref[d].astype(F32)[OWNERS:],
+                jnp.zeros((HALF - ELECS, LANES), F32),
+            ],
+            axis=0,
         )
+        pair = block_diagonal(pair, square).astype(BF16)
+        push_ref[d] = TAU * jnp.dot(push_ref[d].astype(BF16), pair, preferred_element_type=F32)
     moved = [push_ref[:, orbital, :] for orbital in range(ORBS)]
-    wide_ref[...] = bundle_ref[0:OWNERS, 16:32, :].astype(F32)
+    for d in range(OWNERS):
+        wide_ref[d] = drive_ref[d].astype(F32)[OWNERS:]
     for half in range(2):
         for tile in range(TILES):
             out_ref[OWNERS * half:OWNERS * (half + 1), tile * LANES:(tile + 1) * LANES] = (
@@ -327,8 +350,13 @@
     place = places(src_group, own_group, cap)
     rows = call(
         migrate_pack, "migrate_pack", shape((groups * cap, 8, LANES)),
-        (own_group.reshape(1), src_group.reshape(1, -1), src_slot.reshape(1, -1), phi_in),
-        smem() + vmem(3),
+        (own_group.reshape(1), src_group.reshape(1, -1), src_slot, phi_in),
+        smem() + [pl.BlockSpec(memory_space=pltpu.HBM)] * 3,
+        [
+            pltpu.VMEM((1, groups * WALKERS), jnp.int32), pltpu.VMEM((groups * WALKERS,), jnp.int32),
+            pltpu.VMEM((WALKERS, ORBS * ELECS), F32), pltpu.SemaphoreType.DMA((3,)),
+        ],
+        limit=60,
     )
     rows = exchange(rows, "walk")
     owned = call(
@@ -348,29 +376,32 @@
     )
     theta = exchange(theta, "chol")
 
-    def forces(theta, step):
+    def forces(theta, step, corr=(), phi=()):
         force = call(
-            force_kernel, "force", shape((DEVS, OWNERS, LANES), BF16), (theta, lrot), vmem(2), [few]
+            force_kernel, "force", shape((DEVS, OWNERS + 24 * len(corr), LANES), BF16),
+            (theta, lrot, *corr), vmem(2 + len(corr)), [few],
         )
         force = exchange(force, "chol")
         drive, capped = call(
             lambda *refs: drive_kernel(step, *refs), "drive",
-            [shape((DEVS, OWNERS, LANES), BF16), shape((WALKERS, HALF))],
-            (force, fields), vmem(2), [pltpu.VMEM((WALKERS, LANES), F32)],
+            [shape((DEVS, OWNERS + 16 * len(phi), LANES), BF16), shape((WALKERS, HALF))],
+            (force, fields, *phi), vmem(2 + len(phi)), [pltpu.VMEM((WALKERS, LANES), F32)],
         )
-        return exchange(drive, "chol"), capped
-
-    drive, _ = forces(theta, 0)
+        return force, exchange(drive, "chol"), capped
+
+    _, drive, _ = forces(theta, 0)
     push = call(push_kernel, "push", shape((DEVS, 16, LANES), BF16), (drive, lrot), vmem(2), [few])
     push = exchange(push, "chol")
-    bundle = call(
-        owner_next, "owner_next", shape((DEVS, 96, LANES), BF16),
+    theta, phi, corr = call(
+        owner_next, "owner_next",
+        [shape((DEVS, 48, LANES), BF16), shape((DEVS * ORBS, LANES)), shape((HALF, LANES))],
         (push, phi, corr, trial_all), vmem(4), [wide], micros=6.0,
     )
-    bundle = exchange(bundle, "chol")
-    drive, capped = forces(bundle, 1)
+    theta = exchange(theta, "chol")
+    phi = call(phi_pack, "phi_pack", shape((DEVS, 16, LANES), BF16), (phi,), vmem(), [wide])
+    force, drive, capped = forces(theta, 1, (corr,), (phi,))
     phi_out = call(
-        last_kernel, "last", shape((WALKERS, ORBS * ELECS)), (drive, lrot, bundle), vmem(3),
+        last_kernel, "last", shape((WALKERS, ORBS * ELECS)), (drive, lrot, theta, force), vmem(4),
         [few, few],
     )
     return phi_out, capped

time: 181 us -> 176 us (0.972)
  blocking collectives: 136 us -> 115 us
  waiting for transfers between devices: 12 us -> 23.6 us
  starting transfers between devices: 10.4 us -> 15.3 us
  local copies, waits for them, and re-layouts: 3.07 us -> 0.78 us
    all_to_all x8 -> x7, blocking collectives: 136 us -> 115 us  [exchange(): return lax.all_to_all(flat, axis, 0, 0, tiled=True).reshape(array.shape)]
    all_to_all x1 -> x2, waiting for transfers between devices: 12 us -> 23.6 us  [exchange(): return lax.all_to_all(flat, axis, 0, 0, tiled=True).reshape(array.shape)]
    all_to_all x1 -> x2, starting transfers between devices: 10.4 us -> 15.3 us  [exchange(): return lax.all_to_all(flat, axis, 0, 0, tiled=True).reshape(array.shape)]
    pallas_call x10 -> x11, Pallas kernels: 17.4 us -> 18.8 us  [call(): pl.pallas_call(kernel, out_shape=listed, in_specs=in_specs, out_specs=vme...]
  transfers between devices with their start and end apart: 1 -> 2, of which waited for: 1 -> 2; matrix products, arithmetic and copies ran while one was open for 1% -> 1% of each run, Pallas kernels for 0% -> 0%
where the time goes in v3:
time: 176 us; the launch traced here: 175 us
  blocking collectives  115 us (65%)
  waiting for transfers between devices  23.6 us (13%)
  Pallas kernels  18.8 us (11%)
  starting transfers between devices  15.3 us (9%)
    all_to_all x7, blocking collectives, exchange(): return lax.all_to_all(flat, axis, 0, 0, tiled=True).reshape(array.shape)  115 us
    all_to_all x2, waiting for transfers between devices, exchange(): return lax.all_to_all(flat, axis, 0, 0, tiled=True).reshape(array.shape)  23.6 us
    pallas_call x11, Pallas kernels, call(): pl.pallas_call(kernel, out_shape=listed, in_specs=in_specs, out_specs=vme...  18.8 us
    all_to_all x2, starting transfers between devices, exchange(): return lax.all_to_all(flat, axis, 0, 0, tiled=True).reshape(array.shape)  15.3 us
  transfers between devices with their start and end apart: 2, of which 2 were waited for; matrix products, arithmetic and copies ran while one was open for 1% of the time, Pallas kernels for 0%

profile of v3, /device:TPU:8, one launch (start us, length us, event | category | flops | bytes accessed | tf_op | source)
XLA Modules:
  0.0 175.4 jit_solution(1278118414440147604)
XLA Ops:
  0.6 0.0 copy-start.3
  0.6 2.6 %migrate_pack.1 = f32[96,8,128]{2,1,0:T(8,128)} custom-call(s32[1]{0:T(128)} %bitcast.1.group_ref, s32[1,768]{1,0:T(1,128)} %bitcast.10, s32[768]{0:T(1024)} %slot_hbm.1, f32[48,896]{1,0:T(8,128)} %phi_hbm.1), custom_call_target="tpu_custom_call" | custom-call | flops 1000000000 | tf_op jit(solution)/shard_map/migrate_pack/pallas_call | solution.py:318
  3.3 10.4 %all-to-all-start = ((f32[16,48,128]{2,1,0:T(8,128)}), f32[16,48,128]{2,1,0:T(8,128)S(1)}, u32[]{:S(2)}, u32[]{:S(2)}) async-start(f32[16,48,128]{2,1,0:T(8,128)} %bitcast.9), calls=%async_computation | async-start | bytes 786432 | tf_op jit(solution)/shard_map/all_to_all | solution.py:337
  13.7 0.8 dynamic-slice_bitcast_fusion
  14.5 0.2 convert_reduce_fusion
  14.7 0.8 multiply_add_fusion.place_ref
  15.4 12.0 %all-to-all-done = f32[16,48,128]{2,1,0:T(8,128)S(1)} async-done(((f32[16,48,128]{2,1,0:T(8,128)}), f32[16,48,128]{2,1,0:T(8,128)S(1)}, u32[]{:S(2)}, u32[]{:S(2)}) %all-to-all-start) | async-done | bytes 393248 | tf_op jit(solution)/shard_map/all_to_all | solution.py:337
  27.4 0.0 copy-done.3
  27.4 0.6 owner_pack.1
  28.0 25.3 %all_to_all.57.in_ref = f32[32,24,128]{2,1,0:T(8,128)S(1)} all-to-all(f32[32,24,128]{2,1,0:T(8,128)S(1)} %owner_pack.1), channel_id=1, replica_groups=mesh['walk'=16,'chol'=32] {'chol'}, dimensions={0} | all-to-all | bytes 786432 | tf_op jit(solution)/shard_map/all_to_all | solution.py:337
  53.3 0.0 copy-start
  53.3 3.6 %owner_first.1 = (bf16[32,16,128]{2,1,0:T(8,128)(2,1)S(1)}, f32[512,128]{1,0:T(8,128)S(1)}, f32[64,128]{1,0:T(8,128)S(1)}, f32[256,128]{1,0:T(8,128)S(1)}) custom-call(f32[32,24,128]{2,1,0:T(8,128)S(1)} %all_to_all.57.in_ref), custom_call_target="tpu_custom_call" | custom-call | flops 6000000000 | tf_op jit(solution)/shard_map/owner_first/pallas_call | solution.py:318
  56.9 0.0 copy-start.2
  56.9 15.2 %all_to_all.58.theta_ref = bf16[32,16,128]{2,1,0:T(8,128)(2,1)S(1)} all-to-all(bf16[32,16,128]{2,1,0:T(8,128)(2,1)S(1)} %get-tuple-element.12), channel_id=1, replica_groups=mesh['walk'=16,'chol'=32] {'chol'}, dimensions={0} | all-to-all | bytes 262144 | tf_op jit(solution)/shard_map/all_to_all | solution.py:337
  72.1 0.0 copy-done
  72.1 0.8 force.2
  72.9 14.3 %all_to_all.59.refs_0_ = bf16[32,24,128]{2,1,0:T(8,128)(2,1)S(1)} all-to-all(bf16[32,24,128]{2,1,0:T(8,128)(2,1)S(1)} %force.2), channel_id=1, replica_groups=mesh['walk'=16,'chol'=32] {'chol'}, dimensions={0} | all-to-all | bytes 393216 | tf_op jit(solution)/shard_map/all_to_all | solution.py:337
  87.2 0.0 copy-done.2
  87.2 0.7 drive.2
  88.0 14.4 %all_to_all.60.drive_ref = bf16[32,24,128]{2,1,0:T(8,128)(2,1)S(1)} all-to-all(bf16[32,24,128]{2,1,0:T(8,128)(2,1)S(1)} %get-tuple-element.13), channel_id=1, replica_groups=mesh['walk'=16,'chol'=32] {'chol'}, dimensions={0} | all-to-all | bytes 393216 | tf_op jit(solution)/shard_map/all_to_all | solution.py:337
  102.3 1.3 push.1
  103.6 13.9 %all_to_all.61.push_ref = bf16[32,16,128]{2,1,0:T(8,128)(2,1)S(1)} all-to-all(bf16[32,16,128]{2,1,0:T(8,128)(2,1)S(1)} %push.1), channel_id=1, replica_groups=mesh['walk'=16,'chol'=32] {'chol'}, dimensions={0} | all-to-all | bytes 262144 | tf_op jit(solution)/shard_map/all_to_all | solution.py:337
  117.5 4.0 %owner_next.1 = (bf16[32,48,128]{2,1,0:T(8,128)(2,1)S(1)}, f32[512,128]{1,0:T(8,128)S(1)}, f32[64,128]{1,0:T(8,128)S(1)}) custom-call(bf16[32,16,128]{2,1,0:T(8,128)(2,1)S(1)} %all_to_all.61.push_ref, f32[512,128]{1,0:T(8,128)S(1)} %get-tuple-element.14.phi_ref, f32[64,128]{1,0:T(8,128)S(1)} %get-tuple-element.15.corr_ref, ...), custom_call_target="tpu_custom_call" | custom-call | flops 6000000000 | tf_op jit(solution)/shard_map/owner_next/pallas_call | solution.py:318
  121.5 16.2 %all_to_all.62.theta_ref = bf16[32,48,128]{2,1,0:T(8,128)(2,1)S(1)} all-to-all(bf16[32,48,128]{2,1,0:T(8,128)(2,1)S(1)} %get-tuple-element.17), channel_id=1, replica_groups=mesh['walk'=16,'chol'=32] {'chol'}, dimensions={0} | all-to-all | bytes 786432 | tf_op jit(solution)/shard_map/all_to_all | solution.py:337
  137.7 1.6 force.3
  139.2 4.9 %all-to-all-start.7 = ((bf16[32,48,128]{2,1,0:T(8,128)(2,1)}), bf16[32,48,128]{2,1,0:T(8,128)(2,1)S(1)}, u32[]{:S(2)}, u32[]{:S(2)}) async-start(bf16[32,48,128]{2,1,0:T(8,128)(2,1)} %force.3), calls=%async_computation.7 | async-start | bytes 786432 | tf_op jit(solution)/shard_map/all_to_all | solution.py:337
  144.1 0.2 phi_pack.1.refs_2_
  144.3 11.6 %all-to-all-done.7.refs_0_.force_ref = bf16[32,48,128]{2,1,0:T(8,128)(2,1)S(1)} async-done(((bf16[32,48,128]{2,1,0:T(8,128)(2,1)}), bf16[32,48,128]{2,1,0:T(8,128)(2,1)S(1)}, u32[]{:S(2)}, u32[]{:S(2)}) %all-to-all-start.7) | async-done | bytes 393248 | tf_op jit(solution)/shard_map/all_to_all | solution.py:337
  155.9 0.7 drive.3
  156.7 16.1 %all_to_all.63.drive_ref = bf16[32,40,128]{2,1,0:T(8,128)(2,1)S(1)} all-to-all(bf16[32,40,128]{2,1,0:T(8,128)(2,1)S(1)} %get-tuple-element.20), channel_id=1, replica_groups=mesh['walk'=16,'chol'=32] {'chol'}, dimensions={0} | all-to-all | bytes 655360 | tf_op jit(solution)/shard_map/all_to_all | solution.py:337
  172.8 0.0 copy-done.1
  172.8 2.6 %last.1 = f32[48,896]{1,0:T(8,128)} custom-call(bf16[32,40,128]{2,1,0:T(8,128)(2,1)S(1)} %all_to_all.63.drive_ref, bf16[896,2048]{1,0:T(8,128)(2,1)S(1)} %copy-done.1, bf16[32,48,128]{2,1,0:T(8,128)(2,1)S(1)} %all_to_all.62.theta_ref, bf16[32,48,128]{2,1,0:T(8,128)(2,1)S(1)} %all-to-all-done.7.refs_0_.force_ref), custom_call_target="tpu_custom_call" | custom-call | flops 1000000000 | tf_op jit(solution)/shard_map/last/pallas_call | solution.py:318
  (1 shorter events, 0.0 us)
Async XLA Ops:
  0.6 26.8 %copy-start.3 = (f32[16,56]{1,0:T(8,128)S(1)}, f32[16,56]{1,0:T(8,128)}, u32[]{:S(2)}) copy-start(f32[16,56]{1,0:T(8,128)} %trial_ref.1) | copy-start | bytes 10756
  3.3 24.1 %all-to-all-start = ((f32[16,48,128]{2,1,0:T(8,128)}), f32[16,48,128]{2,1,0:T(8,128)S(1)}, u32[]{:S(2)}, u32[]{:S(2)}) async-start(f32[16,48,128]{2,1,0:T(8,128)} %bitcast.9), calls=%async_computation | async-start | bytes 786432 | tf_op jit(solution)/shard_map/all_to_all | solution.py:337
  53.3 18.7 %copy-start = (bf16[896,2048]{1,0:T(8,128)(2,1)S(1)}, bf16[896,2048]{1,0:T(8,128)(2,1)}, u32[]{:S(2)}) copy-start(bf16[896,2048]{1,0:T(8,128)(2,1)} %lrot_ref.7) | copy-start | bytes 11010052
  56.9 30.3 %copy-start.2 = (f32[2,48,64]{2,1,0:T(8,128)S(1)}, f32[2,48,64]{2,1,0:T(8,128)}, u32[]{:S(2)}) copy-start(f32[2,48,64]{2,1,0:T(8,128)} %refs_1_.3) | copy-start | bytes 73732
  139.2 16.7 %all-to-all-start.7 = ((bf16[32,48,128]{2,1,0:T(8,128)(2,1)}), bf16[32,48,128]{2,1,0:T(8,128)(2,1)S(1)}, u32[]{:S(2)}, u32[]{:S(2)}) async-start(bf16[32,48,128]{2,1,0:T(8,128)(2,1)} %force.3), calls=%async_computation.7 | async-start | bytes 786432 | tf_op jit(solution)/shard_map/all_to_all | solution.py:337
  155.9 16.9 %copy-start.1 = (bf16[896,2048]{1,0:T(8,128)(2,1)S(1)}, bf16[896,2048]{1,0:T(8,128)(2,1)}, u32[]{:S(2)}) copy-start(bf16[896,2048]{1,0:T(8,128)(2,1)} %lrot_ref.7) | copy-start | bytes 11010052

commit v4 on v3

--- a/solution.py
+++ b/solution.py
@@ -43,6 +43,21 @@
     return lax.dot_general(
         left, right, (((left_dim,), (right_dim,)), ((), ())),
         precision=EXACT, preferred_element_type=F32,
+    )
+
+
+def parts(value):
+    high = value.astype(BF16)
+    return high, (value - high.astype(F32)).astype(BF16)
+
+
+def near_dot(left, right):
+    left_high, left_low = parts(left)
+    right_high, right_low = parts(right)
+    return jnp.dot(
+        jnp.concatenate([left_high, left_high, left_low], axis=1),
+        jnp.concatenate([right_high, right_low, right_high], axis=0),
+        preferred_element_type=F32,
     )
 
 
@@ -105,9 +120,8 @@
 
 def correlate(trial, walkers):
     rows = DEVS * ORBS // 2
-    low = exact_dot(trial, walkers[:rows], 0, 0)
-    high = exact_dot(trial, walkers[rows:], 0, 0)
-    return low[:HALF] + high[HALF:]
+    both = near_dot(trial, jnp.concatenate([walkers[:rows], walkers[rows:]], axis=1))
+    return both[:HALF, :LANES] + both[HALF:, LANES:]
 
 
 def theta_blocks(walkers, correlation):
@@ -117,7 +131,7 @@
     inverse_gram = invert_pair(packed)
     inverse_gram = jnp.concatenate([inverse_gram, jnp.zeros((HALF - ELECS, LANES), F32)], axis=0)
     inverse = exact_dot(block_diagonal(inverse_gram, lanes), block_diagonal(correlation, lanes), 1, 1)
-    theta = exact_dot(walkers, inverse, 1, 0)
+    theta = near_dot(walkers, inverse)
     return [theta[DEVS * a:DEVS * (a + 1)] for a in range(ORBS)]
 
 
@@ -181,7 +195,7 @@
     lanes = lane_ids(DEVS)
     tiles = [[in_ref[:, 8 * h + k, :] for k in range(TILES)] for h in range(2)]
     walkers = jnp.concatenate(pack_pair(tiles[0], tiles[1], lanes), axis=0)
-    trial = jnp.concatenate([in_ref[:, 16 + k, :] for k in range(8)], axis=0)
+    trial = jnp.concatenate([in_ref[:, 16 + k, :] for k in range(8)], axis=0).T
     correlation = correlate(trial, walkers)
     phi_ref[...] = walkers
     corr_ref[...] = correlation
@@ -194,20 +208,19 @@
     wide_ref[...] = push_ref[...].astype(F32)
     tiles = [[wide_ref[:, 8 * h + k, :] for k in range(TILES)] for h in range(2)]
     push = jnp.concatenate(pack_pair(tiles[0], tiles[1], lanes), axis=0)
-    old = block_diagonal(corr_ref[...], lane_ids(HALF))
-    walkers = phi_ref[...] + TAU * exact_dot(push, old, 1, 0)
+    high, low = parts(block_diagonal(corr_ref[...], lane_ids(HALF)))
+    moved = jnp.dot(
+        push.astype(BF16), jnp.concatenate([high, low], axis=1), preferred_element_type=F32
+    )
+    walkers = phi_ref[...] + TAU * (moved[:, :LANES] + moved[:, LANES:])
     correlation = correlate(trial_ref[...], walkers)
-    next_phi_ref[...] = walkers
     next_corr_ref[...] = correlation
+    blocks = [walkers[DEVS * a:DEVS * (a + 1)] for a in range(ORBS)]
+    store_walkers(blocks, wide_ref, next_phi_ref)
     store_walkers(theta_blocks(walkers, correlation), wide_ref, out_ref)
     sent = correlation[0:32].astype(BF16)
     for d in range(DEVS):
         out_ref[d, 16:48, :] = sent
-
-
-def phi_pack(phi_ref, out_ref, wide_ref):
-    blocks = [phi_ref[DEVS * a:DEVS * (a + 1), :] for a in range(ORBS)]
-    store_walkers(blocks, wide_ref, out_ref)
 
 
 def force_kernel(theta_ref, lrot_ref, *refs):
@@ -370,7 +383,7 @@
         owner_first, "owner_first",
         [
             shape((DEVS, 16, LANES), BF16), shape((DEVS * ORBS, LANES)),
-            shape((HALF, LANES)), shape((DEVS * ORBS // 2, LANES)),
+            shape((HALF, LANES)), shape((LANES, DEVS * ORBS // 2)),
         ],
         (owned,), vmem(), [wide], micros=6.0,
     )
@@ -394,11 +407,10 @@
     push = exchange(push, "chol")
     theta, phi, corr = call(
         owner_next, "owner_next",
-        [shape((DEVS, 48, LANES), BF16), shape((DEVS * ORBS, LANES)), shape((HALF, LANES))],
+        [shape((DEVS, 48, LANES), BF16), shape((DEVS, 16, LANES), BF16), shape((HALF, LANES))],
         (push, phi, corr, trial_all), vmem(4), [wide], micros=6.0,
     )
     theta = exchange(theta, "chol")
-    phi = call(phi_pack, "phi_pack", shape((DEVS, 16, LANES), BF16), (phi,), vmem(), [wide])
     force, drive, capped = forces(theta, 1, (corr,), (phi,))
     phi_out = call(
         last_kernel, "last", shape((WALKERS, ORBS * ELECS)), (drive, lrot, theta, force), vmem(4),

time: 176 us -> 174 us (0.989)
  blocking collectives: 115 us -> 132 us
  waiting for transfers between devices: 23.6 us -> 12 us
  starting transfers between devices: 15.3 us -> 10.4 us
  Pallas kernels: 18.8 us -> 16.9 us
    all_to_all x7 -> x8, blocking collectives: 115 us -> 132 us  [exchange(): return lax.all_to_all(flat, axis, 0, 0, tiled=True).reshape(array.shape)]
    all_to_all x2 -> x1, waiting for transfers between devices: 23.6 us -> 12 us  [exchange(): return lax.all_to_all(flat, axis, 0, 0, tiled=True).reshape(array.shape)]
    all_to_all x2 -> x1, starting transfers between devices: 15.3 us -> 10.4 us  [exchange(): return lax.all_to_all(flat, axis, 0, 0, tiled=True).reshape(array.shape)]
    pallas_call x11 -> x10, Pallas kernels: 18.8 us -> 16.9 us  [call(): pl.pallas_call(kernel, out_shape=listed, in_specs=in_specs, out_specs=vme...]
  transfers between devices with their start and end apart: 2 -> 1, of which waited for: 2 -> 1; matrix products, arithmetic and copies ran while one was open for 1% -> 1% of each run, Pallas kernels for 0% -> 0%
where the time goes in v4:
time: 174 us
  blocking collectives  132 us (76%)
  Pallas kernels  16.9 us (10%)
  waiting for transfers between devices  12 us (7%)
  starting transfers between devices  10.4 us (6%)
    all_to_all x8, blocking collectives, exchange(): return lax.all_to_all(flat, axis, 0, 0, tiled=True).reshape(array.shape)  132 us
    pallas_call x10, Pallas kernels, call(): pl.pallas_call(kernel, out_shape=listed, in_specs=in_specs, out_specs=vme...  16.9 us
    all_to_all x1, waiting for transfers between devices, exchange(): return lax.all_to_all(flat, axis, 0, 0, tiled=True).reshape(array.shape)  12 us
    all_to_all x1, starting transfers between devices, exchange(): return lax.all_to_all(flat, axis, 0, 0, tiled=True).reshape(array.shape)  10.4 us
  transfers between devices with their start and end apart: 1, of which 1 were waited for; matrix products, arithmetic and copies ran while one was open for 1% of the time, Pallas kernels for 0%

profile of v4, /device:TPU:8, one launch (start us, length us, event | category | flops | bytes accessed | tf_op | source)
XLA Modules:
  0.0 173.5 jit_solution(5329358164390070430)
XLA Ops:
  0.6 0.0 copy-start.2
  0.6 2.7 %migrate_pack.1 = f32[96,8,128]{2,1,0:T(8,128)} custom-call(s32[1]{0:T(128)} %bitcast.1.group_ref, s32[1,768]{1,0:T(1,128)} %bitcast.10, s32[768]{0:T(1024)} %slot_hbm.1, f32[48,896]{1,0:T(8,128)} %phi_hbm.1), custom_call_target="tpu_custom_call" | custom-call | flops 1000000000 | tf_op jit(solution)/shard_map/migrate_pack/pallas_call | solution.py:331
  3.3 10.4 %all-to-all-start = ((f32[16,48,128]{2,1,0:T(8,128)}), f32[16,48,128]{2,1,0:T(8,128)S(1)}, u32[]{:S(2)}, u32[]{:S(2)}) async-start(f32[16,48,128]{2,1,0:T(8,128)} %bitcast.9), calls=%async_computation | async-start | bytes 786432 | tf_op jit(solution)/shard_map/all_to_all | solution.py:350
  13.8 0.8 dynamic-slice_bitcast_fusion
  14.5 0.2 convert_reduce_fusion
  14.7 0.8 multiply_add_fusion.place_ref
  15.4 12.0 %all-to-all-done = f32[16,48,128]{2,1,0:T(8,128)S(1)} async-done(((f32[16,48,128]{2,1,0:T(8,128)}), f32[16,48,128]{2,1,0:T(8,128)S(1)}, u32[]{:S(2)}, u32[]{:S(2)}) %all-to-all-start) | async-done | bytes 393248 | tf_op jit(solution)/shard_map/all_to_all | solution.py:350
  27.4 0.0 copy-done.2
  27.4 0.6 owner_pack.1
  28.1 25.3 %all_to_all.57.in_ref = f32[32,24,128]{2,1,0:T(8,128)S(1)} all-to-all(f32[32,24,128]{2,1,0:T(8,128)S(1)} %owner_pack.1), channel_id=1, replica_groups=mesh['walk'=16,'chol'=32] {'chol'}, dimensions={0} | all-to-all | bytes 786432 | tf_op jit(solution)/shard_map/all_to_all | solution.py:350
  53.4 0.0 copy-start
  53.4 3.3 %owner_first.1 = (bf16[32,16,128]{2,1,0:T(8,128)(2,1)S(1)}, f32[512,128]{1,0:T(8,128)S(1)}, f32[64,128]{1,0:T(8,128)S(1)}, f32[128,256]{1,0:T(8,128)S(1)}) custom-call(f32[32,24,128]{2,1,0:T(8,128)S(1)} %all_to_all.57.in_ref), custom_call_target="tpu_custom_call" | custom-call | flops 6000000000 | tf_op jit(solution)/shard_map/owner_first/pallas_call | solution.py:331
  56.7 0.0 copy-start.1
  56.7 15.2 %all_to_all.58.theta_ref = bf16[32,16,128]{2,1,0:T(8,128)(2,1)S(1)} all-to-all(bf16[32,16,128]{2,1,0:T(8,128)(2,1)S(1)} %get-tuple-element.12), channel_id=1, replica_groups=mesh['walk'=16,'chol'=32] {'chol'}, dimensions={0} | all-to-all | bytes 262144 | tf_op jit(solution)/shard_map/all_to_all | solution.py:350
  71.8 0.0 copy-done
  71.8 0.8 force.2
  72.7 14.3 %all_to_all.59.refs_0_ = bf16[32,24,128]{2,1,0:T(8,128)(2,1)S(1)} all-to-all(bf16[32,24,128]{2,1,0:T(8,128)(2,1)S(1)} %force.2), channel_id=1, replica_groups=mesh['walk'=16,'chol'=32] {'chol'}, dimensions={0} | all-to-all | bytes 393216 | tf_op jit(solution)/shard_map/all_to_all | solution.py:350
  87.0 0.0 copy-done.1
  87.0 0.7 drive.2
  87.7 14.5 %all_to_all.60.drive_ref = bf16[32,24,128]{2,1,0:T(8,128)(2,1)S(1)} all-to-all(bf16[32,24,128]{2,1,0:T(8,128)(2,1)S(1)} %get-tuple-element.13), channel_id=1, replica_groups=mesh['walk'=16,'chol'=32] {'chol'}, dimensions={0} | all-to-all | bytes 393216 | tf_op jit(solution)/shard_map/all_to_all | solution.py:350
  102.2 1.3 push.1
  103.5 13.8 %all_to_all.61.push_ref = bf16[32,16,128]{2,1,0:T(8,128)(2,1)S(1)} all-to-all(bf16[32,16,128]{2,1,0:T(8,128)(2,1)S(1)} %push.1), channel_id=1, replica_groups=mesh['walk'=16,'chol'=32] {'chol'}, dimensions={0} | all-to-all | bytes 262144 | tf_op jit(solution)/shard_map/all_to_all | solution.py:350
  117.3 3.4 %owner_next.1 = (bf16[32,48,128]{2,1,0:T(8,128)(2,1)S(1)}, bf16[32,16,128]{2,1,0:T(8,128)(2,1)S(1)}, f32[64,128]{1,0:T(8,128)S(1)}) custom-call(bf16[32,16,128]{2,1,0:T(8,128)(2,1)S(1)} %all_to_all.61.push_ref, f32[512,128]{1,0:T(8,128)S(1)} %get-tuple-element.14.phi_ref, f32[64,128]{1,0:T(8,128)S(1)} %get-tuple-element.15.corr_ref, ...), custom_call_target="tpu_custom_call" | custom-call | flops 6000000000 | tf_op jit(solution)/shard_map/owner_next/pallas_call | solution.py:331
  120.7 16.2 %all_to_all.62.theta_ref = bf16[32,48,128]{2,1,0:T(8,128)(2,1)S(1)} all-to-all(bf16[32,48,128]{2,1,0:T(8,128)(2,1)S(1)} %get-tuple-element.17), channel_id=1, replica_groups=mesh['walk'=16,'chol'=32] {'chol'}, dimensions={0} | all-to-all | bytes 786432 | tf_op jit(solution)/shard_map/all_to_all | solution.py:350
  136.8 0.8 force.3
  137.7 16.5 %all_to_all.63.refs_0_.force_ref = bf16[32,48,128]{2,1,0:T(8,128)(2,1)S(1)} all-to-all(bf16[32,48,128]{2,1,0:T(8,128)(2,1)S(1)} %force.3), channel_id=1, replica_groups=mesh['walk'=16,'chol'=32] {'chol'}, dimensions={0} | all-to-all | bytes 786432 | tf_op jit(solution)/shard_map/all_to_all | solution.py:350
  154.2 0.7 drive.3
  154.9 16.0 %all_to_all.64.drive_ref = bf16[32,40,128]{2,1,0:T(8,128)(2,1)S(1)} all-to-all(bf16[32,40,128]{2,1,0:T(8,128)(2,1)S(1)} %get-tuple-element.20), channel_id=1, replica_groups=mesh['walk'=16,'chol'=32] {'chol'}, dimensions={0} | all-to-all | bytes 655360 | tf_op jit(solution)/shard_map/all_to_all | solution.py:350
  170.9 2.6 %last.1 = f32[48,896]{1,0:T(8,128)} custom-call(bf16[32,40,128]{2,1,0:T(8,128)(2,1)S(1)} %all_to_all.64.drive_ref, bf16[896,2048]{1,0:T(8,128)(2,1)S(1)} %copy-done, bf16[32,48,128]{2,1,0:T(8,128)(2,1)S(1)} %all_to_all.62.theta_ref, bf16[32,48,128]{2,1,0:T(8,128)(2,1)S(1)} %all_to_all.63.refs_0_.force_ref), custom_call_target="tpu_custom_call" | custom-call | flops 1000000000 | tf_op jit(solution)/shard_map/last/pallas_call | solution.py:331
Async XLA Ops:
  0.6 26.8 %copy-start.2 = (f32[16,56]{1,0:T(8,128)S(1)}, f32[16,56]{1,0:T(8,128)}, u32[]{:S(2)}) copy-start(f32[16,56]{1,0:T(8,128)} %trial_ref.1) | copy-start | bytes 10756
  3.3 24.1 %all-to-all-start = ((f32[16,48,128]{2,1,0:T(8,128)}), f32[16,48,128]{2,1,0:T(8,128)S(1)}, u32[]{:S(2)}, u32[]{:S(2)}) async-start(f32[16,48,128]{2,1,0:T(8,128)} %bitcast.9), calls=%async_computation | async-start | bytes 786432 | tf_op jit(solution)/shard_map/all_to_all | solution.py:350
  53.4 18.5 %copy-start = (bf16[896,2048]{1,0:T(8,128)(2,1)S(1)}, bf16[896,2048]{1,0:T(8,128)(2,1)}, u32[]{:S(2)}) copy-start(bf16[896,2048]{1,0:T(8,128)(2,1)} %lrot_ref.7) | copy-start | bytes 11010052
  56.7 30.3 %copy-start.1 = (f32[2,48,64]{2,1,0:T(8,128)S(1)}, f32[2,48,64]{2,1,0:T(8,128)}, u32[]{:S(2)}) copy-start(f32[2,48,64]{2,1,0:T(8,128)} %refs_1_.3) | copy-start | bytes 73732

commit v5 on v4

--- a/solution.py
+++ b/solution.py
@@ -162,8 +162,12 @@
     copies[1].wait()
     held = jnp.where(slot_ids == slot_ref[...].reshape(1, count), 1.0, 0.0).astype(BF16)
     choice = lax.dot_general(taken, held, (((1,), (1,)), ((), ())), preferred_element_type=F32)
+    choice = choice.astype(BF16)
     copies[2].wait()
-    rows = exact_dot(choice, phi_ref[...], 1, 0)
+    phi = phi_ref[...]
+    high, rest = parts(phi)
+    low = (phi - high.astype(F32) - rest.astype(F32)).astype(BF16)
+    rows = sum(jnp.dot(choice, part, preferred_element_type=F32) for part in (high, rest, low))
     for tile in range(TILES):
         out_ref[:, tile, :] = rows[:, tile * LANES:(tile + 1) * LANES]
     out_ref[:, TILES, :] = jnp.zeros((groups * cap, LANES), F32)
@@ -241,8 +245,8 @@
         top, low = block[:OWNERS], block[OWNERS:]
         even = jnp.where(lanes < HALF, top, turn(low, HALF))
         odd = jnp.where(lanes < HALF, turn(top, HALF), low)
-        out_ref[2 * pair] = jnp.concatenate([even] + rest, axis=0).astype(BF16)
-        out_ref[2 * pair + 1] = jnp.concatenate([odd] + rest, axis=0).astype(BF16)
+        out_ref[2 * pair] = jnp.concatenate(rest + [even], axis=0).astype(BF16)
+        out_ref[2 * pair + 1] = jnp.concatenate(rest + [odd], axis=0).astype(BF16)
 
 
 def drive_kernel(step, force_ref, fields_ref, *refs):
@@ -250,7 +254,7 @@
     total = force_ref[0].astype(F32)
     for c in range(1, DEVS):
         total = total + force_ref[c].astype(F32)
-    capped = jnp.clip(20.0 * total[0:OWNERS], -1.0, 1.0)
+    capped = jnp.clip(20.0 * total[-OWNERS:], -1.0, 1.0)
     pad_ref[...] = jnp.zeros_like(pad_ref)
     pad_ref[:, 0:HALF] = fields_ref[step]
     lanes = lane_ids(OWNERS)
@@ -258,7 +262,7 @@
     drive = fields - capped
     for d in range(DEVS):
         rest = [ref[d].astype(F32) for ref in rest_ref]
-        out_ref[d] = jnp.concatenate([drive] + rest, axis=0).astype(BF16)
+        out_ref[d] = jnp.concatenate(rest + [drive], axis=0).astype(BF16)
     capped_ref[0:OWNERS, :] = capped[:, 0:HALF]
     capped_ref[OWNERS:, :] = turn(capped, HALF)[:, 0:HALF]
 
@@ -267,8 +271,8 @@
     lanes = lane_ids(OWNERS)
     tops, lows = [], []
     for pair in range(DEVS // 2):
-        left = drive_ref[2 * pair].astype(F32)[0:OWNERS]
-        right = drive_ref[2 * pair + 1].astype(F32)[0:OWNERS]
+        left = drive_ref[2 * pair].astype(F32)[-OWNERS:]
+        right = drive_ref[2 * pair + 1].astype(F32)[-OWNERS:]
         tops.append(jnp.where(lanes < HALF, left, turn(right, HALF)))
         lows.append(jnp.where(lanes < HALF, turn(left, HALF), right))
     drive = jnp.concatenate(
@@ -293,32 +297,21 @@
 def last_kernel(drive_ref, lrot_ref, theta_ref, force_ref, out_ref, push_ref, wide_ref):
     push = gather_push(drive_ref, lrot_ref)
     lanes = lane_ids(OWNERS)
-    tiles = [
-        [
-            push[OWNERS * h:OWNERS * (h + 1), k * LANES:(k + 1) * LANES]
+    for half in range(2):
+        tiles = [
+            push[OWNERS * half:OWNERS * (half + 1), k * LANES:(k + 1) * LANES]
             for k in range(TILES)
         ]
-        for h in range(2)
-    ]
-    blocks = pack_pair(tiles[0], tiles[1], lanes)
-    for orbital in range(ORBS):
-        push_ref[:, orbital, :] = blocks[orbital]
-    square = lane_ids(HALF)
+        for orbital in range(ORBS):
+            block = take_orbital(tiles, orbital, 0, lanes)
+            push_ref[:, ORBS * half + orbital, :] = jnp.where(lanes < ELECS, block, 0.0)
     for d in range(OWNERS):
-        pair = jnp.concatenate(
-            [
-                theta_ref[d, 16:48, :].astype(F32),
-                force_ref[d].astype(F32)[OWNERS:],
-                jnp.zeros((HALF - ELECS, LANES), F32),
-            ],
-            axis=0,
-        )
-        pair = block_diagonal(pair, square).astype(BF16)
-        push_ref[d] = TAU * jnp.dot(push_ref[d].astype(BF16), pair, preferred_element_type=F32)
-    moved = [push_ref[:, orbital, :] for orbital in range(ORBS)]
-    for d in range(OWNERS):
-        wide_ref[d] = drive_ref[d].astype(F32)[OWNERS:]
+        pair = jnp.concatenate([theta_ref[d, 16:48, :], force_ref[d, 0:32, :]], axis=0)
+        rows = push_ref[d][:, 0:HALF].astype(BF16)
+        push_ref[d] = TAU * jnp.dot(rows, pair, preferred_element_type=F32)
+    wide_ref[...] = drive_ref[0:OWNERS, 0:16, :].astype(F32)
     for half in range(2):
+        moved = [push_ref[:, ORBS * half + orbital, :] for orbital in range(ORBS)]
         for tile in range(TILES):
             out_ref[OWNERS * half:OWNERS * (half + 1), tile * LANES:(tile + 1) * LANES] = (
                 wide_ref[:, 8 * half + tile, :] + unpack_tile(moved, tile, half, lanes)
@@ -414,7 +407,7 @@
     force, drive, capped = forces(theta, 1, (corr,), (phi,))
     phi_out = call(
         last_kernel, "last", shape((WALKERS, ORBS * ELECS)), (drive, lrot, theta, force), vmem(4),
-        [few, few],
+        [pltpu.VMEM((OWNERS, 2 * ORBS, LANES), F32), few],
     )
     return phi_out, capped
 

time: 174 us -> 174 us (level)
  no operation moved by 1% of the time
where the time goes in v5:
time: 174 us; the launch traced here: 173 us
  blocking collectives  132 us (76%)
  Pallas kernels  16.7 us (10%)
  waiting for transfers between devices  12 us (7%)
  starting transfers between devices  10.4 us (6%)
    all_to_all x8, blocking collectives, exchange(): return lax.all_to_all(flat, axis, 0, 0, tiled=True).reshape(array.shape)  132 us
    pallas_call x10, Pallas kernels, call(): pl.pallas_call(kernel, out_shape=listed, in_specs=in_specs, out_specs=vme...  16.7 us
    all_to_all x1, waiting for transfers between devices, exchange(): return lax.all_to_all(flat, axis, 0, 0, tiled=True).reshape(array.shape)  12 us
    all_to_all x1, starting transfers between devices, exchange(): return lax.all_to_all(flat, axis, 0, 0, tiled=True).reshape(array.shape)  10.4 us
  transfers between devices with their start and end apart: 1, of which 1 were waited for; matrix products, arithmetic and copies ran while one was open for 1% of the time, Pallas kernels for 0%

profile of v5, /device:TPU:8, one launch (start us, length us, event | category | flops | bytes accessed | tf_op | source)
XLA Modules:
  0.0 173.3 jit_solution(12532498742350270477)
XLA Ops:
  0.6 0.0 copy-start.2
  0.6 2.6 %migrate_pack.1 = f32[96,8,128]{2,1,0:T(8,128)} custom-call(s32[1]{0:T(128)} %bitcast.1.group_ref, s32[1,768]{1,0:T(1,128)} %bitcast.10, s32[768]{0:T(1024)} %slot_hbm.1, f32[48,896]{1,0:T(8,128)} %phi_hbm.1), custom_call_target="tpu_custom_call" | custom-call | flops 1000000000 | tf_op jit(solution)/shard_map/migrate_pack/pallas_call | solution.py:324
  3.2 10.4 %all-to-all-start = ((f32[16,48,128]{2,1,0:T(8,128)}), f32[16,48,128]{2,1,0:T(8,128)S(1)}, u32[]{:S(2)}, u32[]{:S(2)}) async-start(f32[16,48,128]{2,1,0:T(8,128)} %bitcast.9), calls=%async_computation | async-start | bytes 786432 | tf_op jit(solution)/shard_map/all_to_all | solution.py:343
  13.7 0.8 dynamic-slice_bitcast_fusion
  14.4 0.2 convert_reduce_fusion
  14.6 0.8 multiply_add_fusion.place_ref
  15.4 12.0 %all-to-all-done = f32[16,48,128]{2,1,0:T(8,128)S(1)} async-done(((f32[16,48,128]{2,1,0:T(8,128)}), f32[16,48,128]{2,1,0:T(8,128)S(1)}, u32[]{:S(2)}, u32[]{:S(2)}) %all-to-all-start) | async-done | bytes 393248 | tf_op jit(solution)/shard_map/all_to_all | solution.py:343
  27.4 0.0 copy-done.2
  27.4 0.6 owner_pack.1
  28.0 25.3 %all_to_all.57.in_ref = f32[32,24,128]{2,1,0:T(8,128)S(1)} all-to-all(f32[32,24,128]{2,1,0:T(8,128)S(1)} %owner_pack.1), channel_id=1, replica_groups=mesh['walk'=16,'chol'=32] {'chol'}, dimensions={0} | all-to-all | bytes 786432 | tf_op jit(solution)/shard_map/all_to_all | solution.py:343
  53.3 0.0 copy-start
  53.3 3.3 %owner_first.1 = (bf16[32,16,128]{2,1,0:T(8,128)(2,1)S(1)}, f32[512,128]{1,0:T(8,128)S(1)}, f32[64,128]{1,0:T(8,128)S(1)}, f32[128,256]{1,0:T(8,128)S(1)}) custom-call(f32[32,24,128]{2,1,0:T(8,128)S(1)} %all_to_all.57.in_ref), custom_call_target="tpu_custom_call" | custom-call | flops 6000000000 | tf_op jit(solution)/shard_map/owner_first/pallas_call | solution.py:324
  56.6 0.0 copy-start.1
  56.6 15.2 %all_to_all.58.theta_ref = bf16[32,16,128]{2,1,0:T(8,128)(2,1)S(1)} all-to-all(bf16[32,16,128]{2,1,0:T(8,128)(2,1)S(1)} %get-tuple-element.12), channel_id=1, replica_groups=mesh['walk'=16,'chol'=32] {'chol'}, dimensions={0} | all-to-all | bytes 262144 | tf_op jit(solution)/shard_map/all_to_all | solution.py:343
  71.8 0.0 copy-done
  71.8 0.8 force.2
  72.6 14.3 %all_to_all.59.refs_0_ = bf16[32,24,128]{2,1,0:T(8,128)(2,1)S(1)} all-to-all(bf16[32,24,128]{2,1,0:T(8,128)(2,1)S(1)} %force.2), channel_id=1, replica_groups=mesh['walk'=16,'chol'=32] {'chol'}, dimensions={0} | all-to-all | bytes 393216 | tf_op jit(solution)/shard_map/all_to_all | solution.py:343
  86.9 0.0 copy-done.1
  86.9 0.7 drive.2
  87.6 14.5 %all_to_all.60.drive_ref = bf16[32,24,128]{2,1,0:T(8,128)(2,1)S(1)} all-to-all(bf16[32,24,128]{2,1,0:T(8,128)(2,1)S(1)} %get-tuple-element.13), channel_id=1, replica_groups=mesh['walk'=16,'chol'=32] {'chol'}, dimensions={0} | all-to-all | bytes 393216 | tf_op jit(solution)/shard_map/all_to_all | solution.py:343
  102.2 1.3 push.1
  103.5 13.8 %all_to_all.61.push_ref = bf16[32,16,128]{2,1,0:T(8,128)(2,1)S(1)} all-to-all(bf16[32,16,128]{2,1,0:T(8,128)(2,1)S(1)} %push.1), channel_id=1, replica_groups=mesh['walk'=16,'chol'=32] {'chol'}, dimensions={0} | all-to-all | bytes 262144 | tf_op jit(solution)/shard_map/all_to_all | solution.py:343
  117.2 3.4 %owner_next.1 = (bf16[32,48,128]{2,1,0:T(8,128)(2,1)S(1)}, bf16[32,16,128]{2,1,0:T(8,128)(2,1)S(1)}, f32[64,128]{1,0:T(8,128)S(1)}) custom-call(bf16[32,16,128]{2,1,0:T(8,128)(2,1)S(1)} %all_to_all.61.push_ref, f32[512,128]{1,0:T(8,128)S(1)} %get-tuple-element.14.phi_ref, f32[64,128]{1,0:T(8,128)S(1)} %get-tuple-element.15.corr_ref, ...), custom_call_target="tpu_custom_call" | custom-call | flops 6000000000 | tf_op jit(solution)/shard_map/owner_next/pallas_call | solution.py:324
  120.6 16.2 %all_to_all.62.theta_ref = bf16[32,48,128]{2,1,0:T(8,128)(2,1)S(1)} all-to-all(bf16[32,48,128]{2,1,0:T(8,128)(2,1)S(1)} %get-tuple-element.17), channel_id=1, replica_groups=mesh['walk'=16,'chol'=32] {'chol'}, dimensions={0} | all-to-all | bytes 786432 | tf_op jit(solution)/shard_map/all_to_all | solution.py:343
  136.8 0.8 force.3
  137.6 16.5 %all_to_all.63.refs_0_.force_ref = bf16[32,48,128]{2,1,0:T(8,128)(2,1)S(1)} all-to-all(bf16[32,48,128]{2,1,0:T(8,128)(2,1)S(1)} %force.3), channel_id=1, replica_groups=mesh['walk'=16,'chol'=32] {'chol'}, dimensions={0} | all-to-all | bytes 786432 | tf_op jit(solution)/shard_map/all_to_all | solution.py:343
  154.1 0.7 drive.3
  154.8 16.0 %all_to_all.64.drive_ref = bf16[32,40,128]{2,1,0:T(8,128)(2,1)S(1)} all-to-all(bf16[32,40,128]{2,1,0:T(8,128)(2,1)S(1)} %get-tuple-element.20), channel_id=1, replica_groups=mesh['walk'=16,'chol'=32] {'chol'}, dimensions={0} | all-to-all | bytes 655360 | tf_op jit(solution)/shard_map/all_to_all | solution.py:343
  170.8 2.5 %last.1 = f32[48,896]{1,0:T(8,128)} custom-call(bf16[32,40,128]{2,1,0:T(8,128)(2,1)S(1)} %all_to_all.64.drive_ref, bf16[896,2048]{1,0:T(8,128)(2,1)S(1)} %copy-done, bf16[32,48,128]{2,1,0:T(8,128)(2,1)S(1)} %all_to_all.62.theta_ref, bf16[32,48,128]{2,1,0:T(8,128)(2,1)S(1)} %all_to_all.63.refs_0_.force_ref), custom_call_target="tpu_custom_call" | custom-call | flops 1000000000 | tf_op jit(solution)/shard_map/last/pallas_call | solution.py:324
Async XLA Ops:
  0.6 26.7 %copy-start.2 = (f32[16,56]{1,0:T(8,128)S(1)}, f32[16,56]{1,0:T(8,128)}, u32[]{:S(2)}) copy-start(f32[16,56]{1,0:T(8,128)} %trial_ref.1) | copy-start | bytes 10756
  3.2 24.1 %all-to-all-start = ((f32[16,48,128]{2,1,0:T(8,128)}), f32[16,48,128]{2,1,0:T(8,128)S(1)}, u32[]{:S(2)}, u32[]{:S(2)}) async-start(f32[16,48,128]{2,1,0:T(8,128)} %bitcast.9), calls=%async_computation | async-start | bytes 786432 | tf_op jit(solution)/shard_map/all_to_all | solution.py:343
  53.3 18.5 %copy-start = (bf16[896,2048]{1,0:T(8,128)(2,1)S(1)}, bf16[896,2048]{1,0:T(8,128)(2,1)}, u32[]{:S(2)}) copy-start(bf16[896,2048]{1,0:T(8,128)(2,1)} %lrot_ref.7) | copy-start | bytes 11010052
  56.6 30.3 %copy-start.1 = (f32[2,48,64]{2,1,0:T(8,128)S(1)}, f32[2,48,64]{2,1,0:T(8,128)}, u32[]{:S(2)}) copy-start(f32[2,48,64]{2,1,0:T(8,128)} %refs_1_.3) | copy-start | bytes 73732

commit v6 on v5

--- a/solution.py
+++ b/solution.py
@@ -251,10 +251,10 @@
 
 def drive_kernel(step, force_ref, fields_ref, *refs):
     *rest_ref, out_ref, capped_ref, pad_ref = refs
-    total = force_ref[0].astype(F32)
-    for c in range(1, DEVS):
-        total = total + force_ref[c].astype(F32)
-    capped = jnp.clip(20.0 * total[-OWNERS:], -1.0, 1.0)
+    terms = [force_ref[c].astype(F32)[-OWNERS:] for c in range(DEVS)]
+    while len(terms) > 1:
+        terms = [terms[i] + terms[i + 1] for i in range(0, len(terms), 2)]
+    capped = jnp.clip(20.0 * terms[0], -1.0, 1.0)
     pad_ref[...] = jnp.zeros_like(pad_ref)
     pad_ref[:, 0:HALF] = fields_ref[step]
     lanes = lane_ids(OWNERS)

time: 174 us -> 174 us (level)
  no operation moved by 1% of the time
where the time goes in v6:
time: 174 us; the launch traced here: 173 us
  blocking collectives  132 us (76%)
  Pallas kernels  16.7 us (10%)
  waiting for transfers between devices  12 us (7%)
  starting transfers between devices  10.4 us (6%)
    all_to_all x8, blocking collectives, exchange(): return lax.all_to_all(flat, axis, 0, 0, tiled=True).reshape(array.shape)  132 us
    pallas_call x10, Pallas kernels, call(): pl.pallas_call(kernel, out_shape=listed, in_specs=in_specs, out_specs=vme...  16.7 us
    all_to_all x1, waiting for transfers between devices, exchange(): return lax.all_to_all(flat, axis, 0, 0, tiled=True).reshape(array.shape)  12 us
    all_to_all x1, starting transfers between devices, exchange(): return lax.all_to_all(flat, axis, 0, 0, tiled=True).reshape(array.shape)  10.4 us
  transfers between devices with their start and end apart: 1, of which 1 were waited for; matrix products, arithmetic and copies ran while one was open for 1% of the time, Pallas kernels for 0%

profile of v6, /device:TPU:8, one launch (start us, length us, event | category | flops | bytes accessed | tf_op | source)
XLA Modules:
  0.0 173.3 jit_solution(16037865803756682067)
XLA Ops:
  0.6 0.0 copy-start.2
  0.6 2.6 %migrate_pack.1 = f32[96,8,128]{2,1,0:T(8,128)} custom-call(s32[1]{0:T(128)} %bitcast.1.group_ref, s32[1,768]{1,0:T(1,128)} %bitcast.10, s32[768]{0:T(1024)} %slot_hbm.1, f32[48,896]{1,0:T(8,128)} %phi_hbm.1), custom_call_target="tpu_custom_call" | custom-call | flops 1000000000 | tf_op jit(solution)/shard_map/migrate_pack/pallas_call | solution.py:324
  3.2 10.4 %all-to-all-start = ((f32[16,48,128]{2,1,0:T(8,128)}), f32[16,48,128]{2,1,0:T(8,128)S(1)}, u32[]{:S(2)}, u32[]{:S(2)}) async-start(f32[16,48,128]{2,1,0:T(8,128)} %bitcast.9), calls=%async_computation | async-start | bytes 786432 | tf_op jit(solution)/shard_map/all_to_all | solution.py:343
  13.7 0.8 dynamic-slice_bitcast_fusion
  14.4 0.2 convert_reduce_fusion
  14.6 0.8 multiply_add_fusion.place_ref
  15.4 12.0 %all-to-all-done = f32[16,48,128]{2,1,0:T(8,128)S(1)} async-done(((f32[16,48,128]{2,1,0:T(8,128)}), f32[16,48,128]{2,1,0:T(8,128)S(1)}, u32[]{:S(2)}, u32[]{:S(2)}) %all-to-all-start) | async-done | bytes 393248 | tf_op jit(solution)/shard_map/all_to_all | solution.py:343
  27.4 0.0 copy-done.2
  27.4 0.6 owner_pack.1
  28.0 25.3 %all_to_all.57.in_ref = f32[32,24,128]{2,1,0:T(8,128)S(1)} all-to-all(f32[32,24,128]{2,1,0:T(8,128)S(1)} %owner_pack.1), channel_id=1, replica_groups=mesh['walk'=16,'chol'=32] {'chol'}, dimensions={0} | all-to-all | bytes 786432 | tf_op jit(solution)/shard_map/all_to_all | solution.py:343
  53.3 0.0 copy-start
  53.3 3.3 %owner_first.1 = (bf16[32,16,128]{2,1,0:T(8,128)(2,1)S(1)}, f32[512,128]{1,0:T(8,128)S(1)}, f32[64,128]{1,0:T(8,128)S(1)}, f32[128,256]{1,0:T(8,128)S(1)}) custom-call(f32[32,24,128]{2,1,0:T(8,128)S(1)} %all_to_all.57.in_ref), custom_call_target="tpu_custom_call" | custom-call | flops 6000000000 | tf_op jit(solution)/shard_map/owner_first/pallas_call | solution.py:324
  56.6 0.0 copy-start.1
  56.6 15.2 %all_to_all.58.theta_ref = bf16[32,16,128]{2,1,0:T(8,128)(2,1)S(1)} all-to-all(bf16[32,16,128]{2,1,0:T(8,128)(2,1)S(1)} %get-tuple-element.12), channel_id=1, replica_groups=mesh['walk'=16,'chol'=32] {'chol'}, dimensions={0} | all-to-all | bytes 262144 | tf_op jit(solution)/shard_map/all_to_all | solution.py:343
  71.8 0.0 copy-done
  71.8 0.8 force.2
  72.6 14.3 %all_to_all.59.refs_0_ = bf16[32,24,128]{2,1,0:T(8,128)(2,1)S(1)} all-to-all(bf16[32,24,128]{2,1,0:T(8,128)(2,1)S(1)} %force.2), channel_id=1, replica_groups=mesh['walk'=16,'chol'=32] {'chol'}, dimensions={0} | all-to-all | bytes 393216 | tf_op jit(solution)/shard_map/all_to_all | solution.py:343
  86.9 0.0 copy-done.1
  86.9 0.7 drive.2
  87.6 14.5 %all_to_all.60.drive_ref = bf16[32,24,128]{2,1,0:T(8,128)(2,1)S(1)} all-to-all(bf16[32,24,128]{2,1,0:T(8,128)(2,1)S(1)} %get-tuple-element.13), channel_id=1, replica_groups=mesh['walk'=16,'chol'=32] {'chol'}, dimensions={0} | all-to-all | bytes 393216 | tf_op jit(solution)/shard_map/all_to_all | solution.py:343
  102.2 1.3 push.1
  103.4 13.8 %all_to_all.61.push_ref = bf16[32,16,128]{2,1,0:T(8,128)(2,1)S(1)} all-to-all(bf16[32,16,128]{2,1,0:T(8,128)(2,1)S(1)} %push.1), channel_id=1, replica_groups=mesh['walk'=16,'chol'=32] {'chol'}, dimensions={0} | all-to-all | bytes 262144 | tf_op jit(solution)/shard_map/all_to_all | solution.py:343
  117.2 3.4 %owner_next.1 = (bf16[32,48,128]{2,1,0:T(8,128)(2,1)S(1)}, bf16[32,16,128]{2,1,0:T(8,128)(2,1)S(1)}, f32[64,128]{1,0:T(8,128)S(1)}) custom-call(bf16[32,16,128]{2,1,0:T(8,128)(2,1)S(1)} %all_to_all.61.push_ref, f32[512,128]{1,0:T(8,128)S(1)} %get-tuple-element.14.phi_ref, f32[64,128]{1,0:T(8,128)S(1)} %get-tuple-element.15.corr_ref, ...), custom_call_target="tpu_custom_call" | custom-call | flops 6000000000 | tf_op jit(solution)/shard_map/owner_next/pallas_call | solution.py:324
  120.6 16.2 %all_to_all.62.theta_ref = bf16[32,48,128]{2,1,0:T(8,128)(2,1)S(1)} all-to-all(bf16[32,48,128]{2,1,0:T(8,128)(2,1)S(1)} %get-tuple-element.17), channel_id=1, replica_groups=mesh['walk'=16,'chol'=32] {'chol'}, dimensions={0} | all-to-all | bytes 786432 | tf_op jit(solution)/shard_map/all_to_all | solution.py:343
  136.8 0.8 force.3
  137.6 16.5 %all_to_all.63.refs_0_.force_ref = bf16[32,48,128]{2,1,0:T(8,128)(2,1)S(1)} all-to-all(bf16[32,48,128]{2,1,0:T(8,128)(2,1)S(1)} %force.3), channel_id=1, replica_groups=mesh['walk'=16,'chol'=32] {'chol'}, dimensions={0} | all-to-all | bytes 786432 | tf_op jit(solution)/shard_map/all_to_all | solution.py:343
  154.1 0.7 drive.3
  154.8 16.0 %all_to_all.64.drive_ref = bf16[32,40,128]{2,1,0:T(8,128)(2,1)S(1)} all-to-all(bf16[32,40,128]{2,1,0:T(8,128)(2,1)S(1)} %get-tuple-element.20), channel_id=1, replica_groups=mesh['walk'=16,'chol'=32] {'chol'}, dimensions={0} | all-to-all | bytes 655360 | tf_op jit(solution)/shard_map/all_to_all | solution.py:343
  170.8 2.5 %last.1 = f32[48,896]{1,0:T(8,128)} custom-call(bf16[32,40,128]{2,1,0:T(8,128)(2,1)S(1)} %all_to_all.64.drive_ref, bf16[896,2048]{1,0:T(8,128)(2,1)S(1)} %copy-done, bf16[32,48,128]{2,1,0:T(8,128)(2,1)S(1)} %all_to_all.62.theta_ref, bf16[32,48,128]{2,1,0:T(8,128)(2,1)S(1)} %all_to_all.63.refs_0_.force_ref), custom_call_target="tpu_custom_call" | custom-call | flops 1000000000 | tf_op jit(solution)/shard_map/last/pallas_call | solution.py:324
Async XLA Ops:
  0.6 26.7 %copy-start.2 = (f32[16,56]{1,0:T(8,128)S(1)}, f32[16,56]{1,0:T(8,128)}, u32[]{:S(2)}) copy-start(f32[16,56]{1,0:T(8,128)} %trial_ref.1) | copy-start | bytes 10756
  3.2 24.1 %all-to-all-start = ((f32[16,48,128]{2,1,0:T(8,128)}), f32[16,48,128]{2,1,0:T(8,128)S(1)}, u32[]{:S(2)}, u32[]{:S(2)}) async-start(f32[16,48,128]{2,1,0:T(8,128)} %bitcast.9), calls=%async_computation | async-start | bytes 786432 | tf_op jit(solution)/shard_map/all_to_all | solution.py:343
  53.3 18.5 %copy-start = (bf16[896,2048]{1,0:T(8,128)(2,1)S(1)}, bf16[896,2048]{1,0:T(8,128)(2,1)}, u32[]{:S(2)}) copy-start(bf16[896,2048]{1,0:T(8,128)(2,1)} %lrot_ref.7) | copy-start | bytes 11010052
  56.6 30.3 %copy-start.1 = (f32[2,48,64]{2,1,0:T(8,128)S(1)}, f32[2,48,64]{2,1,0:T(8,128)}, u32[]{:S(2)}) copy-start(f32[2,48,64]{2,1,0:T(8,128)} %refs_1_.3) | copy-start | bytes 73732

commit v7 on v5

--- a/solution.py
+++ b/solution.py
@@ -136,7 +136,8 @@
 
 
 def migrate_pack(
-    group_ref, source_hbm, slot_hbm, phi_hbm, out_ref, source_ref, slot_ref, phi_ref, sems
+    group_ref, source_hbm, slot_hbm, phi_hbm, out_hbm, source_ref, slot_ref, phi_ref, out_ref,
+    sems, out_sems,
 ):
     pairs = ((source_hbm, source_ref), (slot_hbm, slot_ref), (phi_hbm, phi_ref))
     copies = [pltpu.make_async_copy(a, b, sems.at[i]) for i, (a, b) in enumerate(pairs)]
@@ -162,15 +163,24 @@
     copies[1].wait()
     held = jnp.where(slot_ids == slot_ref[...].reshape(1, count), 1.0, 0.0).astype(BF16)
     choice = lax.dot_general(taken, held, (((1,), (1,)), ((), ())), preferred_element_type=F32)
-    choice = choice.astype(BF16)
     copies[2].wait()
     phi = phi_ref[...]
     high, rest = parts(phi)
     low = (phi - high.astype(F32) - rest.astype(F32)).astype(BF16)
-    rows = sum(jnp.dot(choice, part, preferred_element_type=F32) for part in (high, rest, low))
-    for tile in range(TILES):
-        out_ref[:, tile, :] = rows[:, tile * LANES:(tile + 1) * LANES]
-    out_ref[:, TILES, :] = jnp.zeros((groups * cap, LANES), F32)
+    size = out_ref.shape[0] // 2
+    sends = []
+    for turn_id in range(2):
+        span = slice(size * turn_id, size * (turn_id + 1))
+        chosen = choice[span].astype(BF16)
+        rows = sum(jnp.dot(chosen, part, preferred_element_type=F32) for part in (high, rest, low))
+        for tile in range(TILES):
+            out_ref[span, tile, :] = rows[:, tile * LANES:(tile + 1) * LANES]
+        out_ref[span, TILES, :] = jnp.zeros((size, LANES), F32)
+        send = pltpu.make_async_copy(out_ref.at[span], out_hbm.at[span], out_sems.at[turn_id])
+        send.start()
+        sends.append(send)
+    for send in sends:
+        send.wait()
 
 
 def owner_pack(place_ref, rows_ref, trial_ref, out_ref, pad_ref):
@@ -318,14 +328,14 @@
             )
 
 
-def call(kernel, name, shapes, operands, in_specs, scratch=(), limit=24, micros=1.0):
+def call(kernel, name, shapes, operands, in_specs, scratch=(), limit=24, micros=1.0, out_space=pltpu.VMEM):
     single = not isinstance(shapes, (list, tuple))
     listed = [shapes] if single else list(shapes)
     result = pl.pallas_call(
         kernel,
         out_shape=listed,
         in_specs=in_specs,
-        out_specs=vmem(len(listed)),
+        out_specs=[pl.BlockSpec(memory_space=out_space)] * len(listed),
         scratch_shapes=list(scratch),
         compiler_params=pltpu.CompilerParams(vmem_limit_bytes=limit * 1024 * 1024),
         cost_estimate=pl.CostEstimate(flops=int(micros * 1e9), bytes_accessed=0, transcendentals=0),
@@ -360,9 +370,10 @@
         smem() + [pl.BlockSpec(memory_space=pltpu.HBM)] * 3,
         [
             pltpu.VMEM((1, groups * WALKERS), jnp.int32), pltpu.VMEM((groups * WALKERS,), jnp.int32),
-            pltpu.VMEM((WALKERS, ORBS * ELECS), F32), pltpu.SemaphoreType.DMA((3,)),
+            pltpu.VMEM((WALKERS, ORBS * ELECS), F32), pltpu.VMEM((groups * cap, 8, LANES), F32),
+            pltpu.SemaphoreType.DMA((3,)), pltpu.SemaphoreType.DMA((2,)),
         ],
-        limit=60,
+        limit=60, out_space=pltpu.HBM,
     )
     rows = exchange(rows, "walk")
     owned = call(

time: 174 us -> 174 us (level)
  no operation moved by 1% of the time
where the time goes in v7:
time: 174 us; the launch traced here: 173 us
  blocking collectives  132 us (76%)
  Pallas kernels  16.7 us (10%)
  waiting for transfers between devices  12 us (7%)
  starting transfers between devices  10.4 us (6%)
    all_to_all x8, blocking collectives, exchange(): return lax.all_to_all(flat, axis, 0, 0, tiled=True).reshape(array.shape)  132 us
    pallas_call x10, Pallas kernels, call(): pl.pallas_call(kernel, out_shape=listed, in_specs=in_specs, out_specs=[pl...  16.7 us
    all_to_all x1, waiting for transfers between devices, exchange(): return lax.all_to_all(flat, axis, 0, 0, tiled=True).reshape(array.shape)  12 us
    all_to_all x1, starting transfers between devices, exchange(): return lax.all_to_all(flat, axis, 0, 0, tiled=True).reshape(array.shape)  10.4 us
  transfers between devices with their start and end apart: 1, of which 1 were waited for; matrix products, arithmetic and copies ran while one was open for 1% of the time, Pallas kernels for 0%

profile of v7, /device:TPU:8, one launch (start us, length us, event | category | flops | bytes accessed | tf_op | source)
XLA Modules:
  0.0 173.4 jit_solution(3230707918284966895)
XLA Ops:
  0.6 0.0 copy-start.2
  0.6 2.6 %migrate_pack.1 = f32[96,8,128]{2,1,0:T(8,128)} custom-call(s32[1]{0:T(128)} %bitcast.1.group_ref, s32[1,768]{1,0:T(1,128)} %bitcast.10, s32[768]{0:T(1024)} %slot_hbm.1, f32[48,896]{1,0:T(8,128)} %phi_hbm.1), custom_call_target="tpu_custom_call" | custom-call | flops 1000000000 | tf_op jit(solution)/shard_map/migrate_pack/pallas_call | solution.py:334
  3.3 10.4 %all-to-all-start = ((f32[16,48,128]{2,1,0:T(8,128)}), f32[16,48,128]{2,1,0:T(8,128)S(1)}, u32[]{:S(2)}, u32[]{:S(2)}) async-start(f32[16,48,128]{2,1,0:T(8,128)} %bitcast.9), calls=%async_computation | async-start | bytes 786432 | tf_op jit(solution)/shard_map/all_to_all | solution.py:353
  13.7 0.8 dynamic-slice_bitcast_fusion
  14.5 0.2 convert_reduce_fusion
  14.6 0.8 multiply_add_fusion.place_ref
  15.4 12.0 %all-to-all-done = f32[16,48,128]{2,1,0:T(8,128)S(1)} async-done(((f32[16,48,128]{2,1,0:T(8,128)}), f32[16,48,128]{2,1,0:T(8,128)S(1)}, u32[]{:S(2)}, u32[]{:S(2)}) %all-to-all-start) | async-done | bytes 393248 | tf_op jit(solution)/shard_map/all_to_all | solution.py:353
  27.4 0.0 copy-done.2
  27.4 0.6 owner_pack.1
  28.0 25.3 %all_to_all.57.in_ref = f32[32,24,128]{2,1,0:T(8,128)S(1)} all-to-all(f32[32,24,128]{2,1,0:T(8,128)S(1)} %owner_pack.1), channel_id=1, replica_groups=mesh['walk'=16,'chol'=32] {'chol'}, dimensions={0} | all-to-all | bytes 786432 | tf_op jit(solution)/shard_map/all_to_all | solution.py:353
  53.3 0.0 copy-start
  53.3 3.3 %owner_first.1 = (bf16[32,16,128]{2,1,0:T(8,128)(2,1)S(1)}, f32[512,128]{1,0:T(8,128)S(1)}, f32[64,128]{1,0:T(8,128)S(1)}, f32[128,256]{1,0:T(8,128)S(1)}) custom-call(f32[32,24,128]{2,1,0:T(8,128)S(1)} %all_to_all.57.in_ref), custom_call_target="tpu_custom_call" | custom-call | flops 6000000000 | tf_op jit(solution)/shard_map/owner_first/pallas_call | solution.py:334
  56.6 0.0 copy-start.1
  56.6 15.2 %all_to_all.58.theta_ref = bf16[32,16,128]{2,1,0:T(8,128)(2,1)S(1)} all-to-all(bf16[32,16,128]{2,1,0:T(8,128)(2,1)S(1)} %get-tuple-element.12), channel_id=1, replica_groups=mesh['walk'=16,'chol'=32] {'chol'}, dimensions={0} | all-to-all | bytes 262144 | tf_op jit(solution)/shard_map/all_to_all | solution.py:353
  71.8 0.0 copy-done
  71.8 0.8 force.2
  72.6 14.3 %all_to_all.59.refs_0_ = bf16[32,24,128]{2,1,0:T(8,128)(2,1)S(1)} all-to-all(bf16[32,24,128]{2,1,0:T(8,128)(2,1)S(1)} %force.2), channel_id=1, replica_groups=mesh['walk'=16,'chol'=32] {'chol'}, dimensions={0} | all-to-all | bytes 393216 | tf_op jit(solution)/shard_map/all_to_all | solution.py:353
  86.9 0.0 copy-done.1
  86.9 0.7 drive.2
  87.7 14.5 %all_to_all.60.drive_ref = bf16[32,24,128]{2,1,0:T(8,128)(2,1)S(1)} all-to-all(bf16[32,24,128]{2,1,0:T(8,128)(2,1)S(1)} %get-tuple-element.13), channel_id=1, replica_groups=mesh['walk'=16,'chol'=32] {'chol'}, dimensions={0} | all-to-all | bytes 393216 | tf_op jit(solution)/shard_map/all_to_all | solution.py:353
  102.2 1.3 push.1
  103.5 13.8 %all_to_all.61.push_ref = bf16[32,16,128]{2,1,0:T(8,128)(2,1)S(1)} all-to-all(bf16[32,16,128]{2,1,0:T(8,128)(2,1)S(1)} %push.1), channel_id=1, replica_groups=mesh['walk'=16,'chol'=32] {'chol'}, dimensions={0} | all-to-all | bytes 262144 | tf_op jit(solution)/shard_map/all_to_all | solution.py:353
  117.2 3.4 %owner_next.1 = (bf16[32,48,128]{2,1,0:T(8,128)(2,1)S(1)}, bf16[32,16,128]{2,1,0:T(8,128)(2,1)S(1)}, f32[64,128]{1,0:T(8,128)S(1)}) custom-call(bf16[32,16,128]{2,1,0:T(8,128)(2,1)S(1)} %all_to_all.61.push_ref, f32[512,128]{1,0:T(8,128)S(1)} %get-tuple-element.14.phi_ref, f32[64,128]{1,0:T(8,128)S(1)} %get-tuple-element.15.corr_ref, ...), custom_call_target="tpu_custom_call" | custom-call | flops 6000000000 | tf_op jit(solution)/shard_map/owner_next/pallas_call | solution.py:334
  120.6 16.2 %all_to_all.62.theta_ref = bf16[32,48,128]{2,1,0:T(8,128)(2,1)S(1)} all-to-all(bf16[32,48,128]{2,1,0:T(8,128)(2,1)S(1)} %get-tuple-element.17), channel_id=1, replica_groups=mesh['walk'=16,'chol'=32] {'chol'}, dimensions={0} | all-to-all | bytes 786432 | tf_op jit(solution)/shard_map/all_to_all | solution.py:353
  136.8 0.8 force.3
  137.6 16.5 %all_to_all.63.refs_0_.force_ref = bf16[32,48,128]{2,1,0:T(8,128)(2,1)S(1)} all-to-all(bf16[32,48,128]{2,1,0:T(8,128)(2,1)S(1)} %force.3), channel_id=1, replica_groups=mesh['walk'=16,'chol'=32] {'chol'}, dimensions={0} | all-to-all | bytes 786432 | tf_op jit(solution)/shard_map/all_to_all | solution.py:353
  154.1 0.7 drive.3
  154.8 16.0 %all_to_all.64.drive_ref = bf16[32,40,128]{2,1,0:T(8,128)(2,1)S(1)} all-to-all(bf16[32,40,128]{2,1,0:T(8,128)(2,1)S(1)} %get-tuple-element.20), channel_id=1, replica_groups=mesh['walk'=16,'chol'=32] {'chol'}, dimensions={0} | all-to-all | bytes 655360 | tf_op jit(solution)/shard_map/all_to_all | solution.py:353
  170.8 2.5 %last.1 = f32[48,896]{1,0:T(8,128)} custom-call(bf16[32,40,128]{2,1,0:T(8,128)(2,1)S(1)} %all_to_all.64.drive_ref, bf16[896,2048]{1,0:T(8,128)(2,1)S(1)} %copy-done, bf16[32,48,128]{2,1,0:T(8,128)(2,1)S(1)} %all_to_all.62.theta_ref, bf16[32,48,128]{2,1,0:T(8,128)(2,1)S(1)} %all_to_all.63.refs_0_.force_ref), custom_call_target="tpu_custom_call" | custom-call | flops 1000000000 | tf_op jit(solution)/shard_map/last/pallas_call | solution.py:334
Async XLA Ops:
  0.6 26.8 %copy-start.2 = (f32[16,56]{1,0:T(8,128)S(1)}, f32[16,56]{1,0:T(8,128)}, u32[]{:S(2)}) copy-start(f32[16,56]{1,0:T(8,128)} %trial_ref.1) | copy-start | bytes 10756
  3.3 24.1 %all-to-all-start = ((f32[16,48,128]{2,1,0:T(8,128)}), f32[16,48,128]{2,1,0:T(8,128)S(1)}, u32[]{:S(2)}, u32[]{:S(2)}) async-start(f32[16,48,128]{2,1,0:T(8,128)} %bitcast.9), calls=%async_computation | async-start | bytes 786432 | tf_op jit(solution)/shard_map/all_to_all | solution.py:353
  53.3 18.5 %copy-start = (bf16[896,2048]{1,0:T(8,128)(2,1)S(1)}, bf16[896,2048]{1,0:T(8,128)(2,1)}, u32[]{:S(2)}) copy-start(bf16[896,2048]{1,0:T(8,128)(2,1)} %lrot_ref.7) | copy-start | bytes 11010052
  56.6 30.3 %copy-start.1 = (f32[2,48,64]{2,1,0:T(8,128)S(1)}, f32[2,48,64]{2,1,0:T(8,128)}, u32[]{:S(2)}) copy-start(f32[2,48,64]{2,1,0:T(8,128)} %refs_1_.3) | copy-start | bytes 73732
